TPU v7x, 32 devices: a whole 2x2x4 slice. The times are simulated.
32 devices in a mesh: seq: 4 (over y, x), batch: 8 (over z, core).
Axes of the slice: x: 2, y: 2, z: 4, core: 2. Of those that a mesh axis runs over, the one named last changes fastest.
Arguments:
- tokens: bfloat16 [32, 1024, 1024], P('batch', 'seq'), may hold values from -6 to 6
- cotangent: bfloat16 [32, 1024, 1024], P('batch', 'seq'), may hold values from -6 to 6
- bins: int32 [32], P('batch'), may hold values from 0 to 63
- live_count: int32 [8], P('batch'), may hold values from 1 to 4, as said below
- w_qkv: bfloat16 [1024, 3072], replicated, may hold values from -0.1875 to 0.1875
- w_out: bfloat16 [1024, 1024], replicated, may hold values from -3.5 to 3.5
- w_up: bfloat16 [1024, 4096], replicated, may hold values from -0.1875 to 0.1875
- w_down: bfloat16 [4096, 1024], replicated, may hold values from -0.09375 to 0.09375
- gain_attn: float32 [64, 1024], replicated, may hold values from 0.1 to 1.9
- gain_mlp: float32 [64, 1024], replicated, may hold values from 0.1 to 1.9
Outputs:
- output: bfloat16 [32, 1024, 1024], P('batch', 'seq')
- grad_tokens: float32 [32, 1024, 1024], P('batch', 'seq')
- grad_qkv: float32 [1024, 3072], P('batch')
- grad_out: float32 [1024, 1024], P('batch')
- grad_up: float32 [1024, 4096], P('batch')
- grad_down: float32 [4096, 1024], P('batch')
- grad_gain_attn: float32 [64, 1024], P('batch')
- grad_gain_mlp: float32 [64, 1024], P('batch')
Inputs may be any that keep to these rules, and one draw needn't show every extreme that they name: The first live_count slots of each index of batch hold live sequences; some index has 4 live and some has 1.
All inputs are finite; a program needn't handle non-finite values.
Results may differ from a plain program's by a relative error of at most 0.015.
Values may be sent and summed in bfloat16 or wider, within the bound.
A program may use at most 256 MiB of HBM per device.

v0:
```python
import math

import jax
import jax.numpy as jnp
from jax import lax
from jax.sharding import PartitionSpec as P

HEADS = 16


def layer_norm(values_in):
    centred = values_in - jnp.mean(values_in, axis=-1, keepdims=True)
    inverse = lax.rsqrt(jnp.mean(centred * centred, axis=-1, keepdims=True) + 1e-05)
    return (centred * inverse, inverse)


def norm_back(grad_normed, normed, inverse):
    first_mean = jnp.mean(grad_normed, axis=-1, keepdims=True)
    second_mean = jnp.mean(grad_normed * normed, axis=-1, keepdims=True)
    return inverse * (grad_normed - first_mean - normed * second_mean)


def weight_grad(left, right):
    return lax.dot_general(
        left, right, (((0,), (0,)), ((), ())), preferred_element_type=jnp.float32
    )


def split_heads(packed, heads_here):
    shaped = packed.reshape(packed.shape[0], heads_here, 3, -1)
    return (shaped[:, :, 0], shaped[:, :, 1], shaped[:, :, 2])


def attend_one(packed, heads_here, block_rows):
    queries, key_rows, values = split_heads(packed, heads_here)
    length, head_size = (queries.shape[0], queries.shape[2])
    factor = head_size ** (-0.5)
    blocked = queries.reshape(length // block_rows, block_rows, heads_here, head_size)

    def per_block(query_block):
        scores = (
            jnp.einsum("qhd,khd->hqk", query_block, key_rows, preferred_element_type=jnp.float32)
            * factor
        )
        row_max = jnp.max(scores, axis=-1, keepdims=True)
        logsum = row_max + jnp.log(jnp.sum(jnp.exp(scores - row_max), axis=-1, keepdims=True))
        softmax_rows = jnp.exp(scores - logsum).astype(jnp.bfloat16)
        mixed_rows = jnp.einsum(
            "hqk,khd->qhd", softmax_rows, values, preferred_element_type=jnp.float32
        )
        return (
            mixed_rows.astype(jnp.bfloat16).reshape(block_rows, heads_here * head_size),
            logsum[..., 0],
        )

    mixed_rows, logsum = lax.map(per_block, blocked)
    return (mixed_rows.reshape(length, heads_here * head_size), logsum)


def attend_back(packed, logsum, grad_mixed, heads_here, block_rows):
    queries, key_rows, values = split_heads(packed, heads_here)
    length, head_size = (queries.shape[0], queries.shape[2])
    factor = head_size ** (-0.5)
    count_blocks = length // block_rows
    query_blocks = queries.reshape(count_blocks, block_rows, heads_here, head_size)
    grad_blocks = grad_mixed.reshape(count_blocks, block_rows, heads_here, head_size)

    def per_block(running, pieces):
        query_block, grad_block, logsum_block = pieces
        scores = (
            jnp.einsum("qhd,khd->hqk", query_block, key_rows, preferred_element_type=jnp.float32)
            * factor
        )
        softmax_rows = jnp.exp(scores - logsum_block[..., None])
        grad_values = running[1] + jnp.einsum(
            "hqk,qhd->khd",
            softmax_rows.astype(jnp.bfloat16),
            grad_block,
            preferred_element_type=jnp.float32,
        )
        grad_soft = jnp.einsum(
            "qhd,khd->hqk", grad_block, values, preferred_element_type=jnp.float32
        )
        inner = jnp.sum(softmax_rows * grad_soft, axis=-1, keepdims=True)
        grad_scores = (softmax_rows * (grad_soft - inner)).astype(jnp.bfloat16)
        grad_query = (
            jnp.einsum("hqk,khd->qhd", grad_scores, key_rows, preferred_element_type=jnp.float32)
            * factor
        )
        grad_keys = (
            running[0]
            + jnp.einsum(
                "hqk,qhd->khd", grad_scores, query_block, preferred_element_type=jnp.float32
            )
            * factor
        )
        return ((grad_keys, grad_values), grad_query)

    zeros_start = jnp.zeros((length, heads_here, head_size), jnp.float32)
    (grad_keys, grad_values), grad_queries = lax.scan(
        per_block, (zeros_start, zeros_start), (query_blocks, grad_blocks, logsum)
    )
    grad_queries = grad_queries.reshape(length, heads_here, head_size)
    stacked = jnp.stack([grad_queries, grad_keys, grad_values], axis=2)
    return stacked.reshape(length, heads_here * 3 * head_size).astype(jnp.bfloat16)


def body(tokens, cotangent, bins, live_count, w_qkv, w_out, w_up, w_down, gain_attn, gain_mlp):
    slot_count, local_rows, model_width = tokens.shape
    seq_ways = lax.axis_size("seq")
    heads_here = HEADS // seq_ways
    length = local_rows * seq_ways
    block_rows = math.gcd(length, 512)
    row_count = slot_count * local_rows
    table_rows = gain_attn.shape[0]
    onehot = (bins[:, None] == jnp.arange(table_rows, dtype=jnp.int32)[None, :]).astype(jnp.float32)
    gains_attn = jnp.dot(onehot, gain_attn, precision=lax.Precision.HIGHEST)[:, None, :]
    gains_mlp = jnp.dot(onehot, gain_mlp, precision=lax.Precision.HIGHEST)[:, None, :]
    inputs = tokens.astype(jnp.float32)

    def attention_part():
        normed_attn, inverse_attn = layer_norm(inputs)
        ready_attn = (normed_attn * gains_attn).astype(jnp.bfloat16).reshape(row_count, model_width)
        packed = jnp.dot(ready_attn, w_qkv, preferred_element_type=jnp.float32).astype(jnp.bfloat16)
        packed = packed.reshape(slot_count, local_rows, 3 * model_width)
        item_rows = lax.all_to_all(packed, "seq", split_axis=2, concat_axis=1, tiled=True)
        mixed_items, logsum_items = lax.map(
            lambda single: attend_one(single, heads_here, block_rows), item_rows
        )
        mixed_rows = lax.all_to_all(
            mixed_items, "seq", split_axis=1, concat_axis=2, tiled=True
        ).reshape(row_count, model_width)
        return (normed_attn, inverse_attn, ready_attn, item_rows, logsum_items, mixed_rows)

    def mlp_part(hidden):
        normed_mlp, inverse_mlp = layer_norm(hidden)
        ready_mlp = (normed_mlp * gains_mlp).astype(jnp.bfloat16).reshape(row_count, model_width)
        upward = jnp.dot(ready_mlp, w_up, preferred_element_type=jnp.float32)
        active = jax.nn.gelu(upward).astype(jnp.bfloat16)
        return (normed_mlp, inverse_mlp, ready_mlp, upward, active)

    saved_attn = attention_part()
    attended = jnp.dot(saved_attn[5], w_out, preferred_element_type=jnp.float32)
    hidden = inputs + attended.reshape(slot_count, local_rows, model_width)
    saved_mlp = mlp_part(hidden)
    branch = jnp.dot(saved_mlp[4], w_down, preferred_element_type=jnp.float32)
    output = (hidden + branch.reshape(slot_count, local_rows, model_width)).astype(jnp.bfloat16)
    saved_attn = attention_part()
    saved_mlp = mlp_part(hidden)
    normed_attn, inverse_attn, ready_attn, packed_heads, logsum, mixed_rows = saved_attn
    normed_mlp, inverse_mlp, ready_mlp, upward, active = saved_mlp
    alive_mask = (jnp.arange(slot_count, dtype=jnp.int32) < live_count[0]).astype(jnp.float32)
    grad_output = cotangent.astype(jnp.float32) * alive_mask[:, None, None]
    low_output = grad_output.astype(jnp.bfloat16).reshape(row_count, model_width)
    grad_down = weight_grad(active, low_output)
    grad_active = jnp.dot(low_output, w_down.T, preferred_element_type=jnp.float32)
    gelu_values, gelu_pull = jax.vjp(jax.nn.gelu, upward)
    grad_upward = gelu_pull(grad_active)[0].astype(jnp.bfloat16)
    grad_up = weight_grad(ready_mlp, grad_upward)
    grad_ready_mlp = jnp.dot(grad_upward, w_up.T, preferred_element_type=jnp.float32).reshape(
        slot_count, local_rows, model_width
    )
    table_mlp = jnp.dot(
        onehot.T, jnp.sum(grad_ready_mlp * normed_mlp, axis=1), precision=lax.Precision.HIGHEST
    )
    grad_hidden = grad_output + norm_back(grad_ready_mlp * gains_mlp, normed_mlp, inverse_mlp)
    low_hidden = grad_hidden.astype(jnp.bfloat16).reshape(row_count, model_width)
    grad_out = weight_grad(mixed_rows, low_hidden)
    grad_mixed = jnp.dot(low_hidden, w_out.T, preferred_element_type=jnp.float32).astype(
        jnp.bfloat16
    )
    grad_mixed = grad_mixed.reshape(slot_count, local_rows, model_width)
    grad_mixed_heads = lax.all_to_all(grad_mixed, "seq", split_axis=2, concat_axis=1, tiled=True)
    grad_packed_heads = lax.map(
        lambda pieces: attend_back(pieces[0], pieces[1], pieces[2], heads_here, block_rows),
        (packed_heads, logsum, grad_mixed_heads),
    )
    grad_packed = lax.all_to_all(
        grad_packed_heads, "seq", split_axis=1, concat_axis=2, tiled=True
    ).reshape(row_count, 3 * model_width)
    grad_qkv = weight_grad(ready_attn, grad_packed)
    grad_ready_attn = jnp.dot(grad_packed, w_qkv.T, preferred_element_type=jnp.float32).reshape(
        slot_count, local_rows, model_width
    )
    table_attn = jnp.dot(
        onehot.T, jnp.sum(grad_ready_attn * normed_attn, axis=1), precision=lax.Precision.HIGHEST
    )
    grad_tokens = grad_hidden + norm_back(grad_ready_attn * gains_attn, normed_attn, inverse_attn)
    gradients = (grad_qkv, grad_out, grad_up, grad_down, table_attn, table_mlp)
    shares = (
        lax.psum_scatter(gradients[0], "batch", scatter_dimension=0, tiled=True),
        lax.psum_scatter(gradients[1], "batch", scatter_dimension=0, tiled=True),
        lax.psum_scatter(gradients[2], "batch", scatter_dimension=0, tiled=True),
        lax.psum_scatter(gradients[3], "batch", scatter_dimension=0, tiled=True),
        lax.psum_scatter(gradients[4], "batch", scatter_dimension=0, tiled=True),
        lax.psum_scatter(gradients[5], "batch", scatter_dimension=0, tiled=True),
    )
    summed = (
        lax.psum(shares[0].astype(jnp.bfloat16), "seq").astype(jnp.float32),
        lax.psum(shares[1].astype(jnp.bfloat16), "seq").astype(jnp.float32),
        lax.psum(shares[2].astype(jnp.bfloat16), "seq").astype(jnp.float32),
        lax.psum(shares[3].astype(jnp.bfloat16), "seq").astype(jnp.float32),
        lax.psum(shares[4].astype(jnp.bfloat16), "seq").astype(jnp.float32),
        lax.psum(shares[5].astype(jnp.bfloat16), "seq").astype(jnp.float32),
    )
    return (output, grad_tokens, summed[0], summed[1], summed[2], summed[3], summed[4], summed[5])


def solution(mesh):
    placed = (
        P("batch", "seq", None),
        P("batch", "seq", None),
        P("batch"),
        P("batch"),
        P(),
        P(),
        P(),
        P(),
        P(),
        P(),
    )
    return jax.shard_map(
        body,
        mesh=mesh,
        in_specs=placed,
        out_specs=(
            P("batch", "seq", None),
            P("batch", "seq", None),
            P("batch", None),
            P("batch", None),
            P("batch", None),
            P("batch", None),
            P("batch", None),
            P("batch", None),
        ),
        check_vma=False,
    )
```

profile of v0, /device:TPU:0, one launch (start us, length us, event | category | flops | bytes accessed | tf_op | source)
XLA Modules:
  0.0 1317.6 jit_solution(15104596651390851997)
XLA Ops:
  43.9 14.5 %fusion.85 = f32[1024,4096]{1,0:T(8,128)} fusion(bf16[1024,1024]{1,0:T(8,128)(2,1)S(1)} %bitcast.272, bf16[4096,1024]{1,0:T(8,128)(2,1)} %param.29), kind=kOutput, calls=%fused_computation.143 | convolution fusion | flops 8589934592 | bytes 27262976 | tf_op jit(solution)/shard_map/dot_general | solution.py:156
  58.4 51.6 %all-to-all-done = bf16[4,256,3072]{1,0,2:T(4,128)(2,1)} async-done(((bf16[4,256,3072]{1,0,2:T(4,128)(2,1)}), bf16[4,256,3072]{1,0,2:T(4,128)(2,1)}, u32[]{:S(2)}, u32[]{:S(2)}) %all-to-all-start) | async-done | bytes 6291488 | tf_op jit(solution)/shard_map/all_to_all | solution.py:126
  132.8 84.4 %while.70 = (s32[]{:T(128)}, bf16[4,1024,256]{2,1,0:T(8,128)(2,1)}, bf16[4,1024,768]{1,2,0:T(8,128)(2,1)}, s32[]{:T(128)}, s32[]{:T(128)}, /*index=5*/s32[]{:T(128)}) while((s32[]{:T(128)}, bf16[4,1024,256]{2,1,0:T(8,128)(2,1)}, bf16[4,1024,768]{1,2,0:T(8,128)(2,1)}, s32[]{:T(128)}, s32[]{:T(128)}, /*index=5*/s32[]{:T(128)}) %tuple.153), condition=%wide.region_7.8_spmd, body=%wide.region_2.7_spmd.sunk | while | flops 553777152 | bytes 37282016 | solution.py:127
  138.2 14.2 %while.75 = (s32[]{:T(128)}, bf16[2,512,256]{2,1,0:T(8,128)(2,1)}, bf16[2,512,4,64]{1,3,2,0:T(8,128)(2,1)}, bf16[1024,4,64]{0,2,1:T(8,128)(2,1)}, bf16[1024,4,64]{0,2,1:T(8,128)(2,1)S(1)}, /*index=5*/s32[]{:T(128)}) while((s32[]{:T(128)}, bf16[2,512,256]{2,1,0:T(8,128)(2,1)}, bf16[2,512,4,64]{1,3,2,0:T(8,128)(2,1)}, ...), condition=%wide.region_6.6_spmd, body=%wide.region_3.5_spmd.sunk | while | flops 553777152 | bytes 27844692 | solution.py:56
  159.2 14.2 %while.75 = (s32[]{:T(128)}, bf16[2,512,256]{2,1,0:T(8,128)(2,1)}, bf16[2,512,4,64]{1,3,2,0:T(8,128)(2,1)}, bf16[1024,4,64]{0,2,1:T(8,128)(2,1)}, bf16[1024,4,64]{0,2,1:T(8,128)(2,1)S(1)}, /*index=5*/s32[]{:T(128)}) while((s32[]{:T(128)}, bf16[2,512,256]{2,1,0:T(8,128)(2,1)}, bf16[2,512,4,64]{1,3,2,0:T(8,128)(2,1)}, ...), condition=%wide.region_6.6_spmd, body=%wide.region_3.5_spmd.sunk | while | flops 553777152 | bytes 27844692 | solution.py:56
  180.2 14.2 %while.75 = (s32[]{:T(128)}, bf16[2,512,256]{2,1,0:T(8,128)(2,1)}, bf16[2,512,4,64]{1,3,2,0:T(8,128)(2,1)}, bf16[1024,4,64]{0,2,1:T(8,128)(2,1)}, bf16[1024,4,64]{0,2,1:T(8,128)(2,1)S(1)}, /*index=5*/s32[]{:T(128)}) while((s32[]{:T(128)}, bf16[2,512,256]{2,1,0:T(8,128)(2,1)}, bf16[2,512,4,64]{1,3,2,0:T(8,128)(2,1)}, ...), condition=%wide.region_6.6_spmd, body=%wide.region_3.5_spmd.sunk | while | flops 553777152 | bytes 27844692 | solution.py:56
  201.2 14.2 %while.75 = (s32[]{:T(128)}, bf16[2,512,256]{2,1,0:T(8,128)(2,1)}, bf16[2,512,4,64]{1,3,2,0:T(8,128)(2,1)}, bf16[1024,4,64]{0,2,1:T(8,128)(2,1)}, bf16[1024,4,64]{0,2,1:T(8,128)(2,1)S(1)}, /*index=5*/s32[]{:T(128)}) while((s32[]{:T(128)}, bf16[2,512,256]{2,1,0:T(8,128)(2,1)}, bf16[2,512,4,64]{1,3,2,0:T(8,128)(2,1)}, ...), condition=%wide.region_6.6_spmd, body=%wide.region_3.5_spmd.sunk | while | flops 553777152 | bytes 27844692 | solution.py:56
  227.8 84.1 %while.72 = (s32[]{:T(128)}, bf16[4,1024,256]{2,1,0:T(8,128)(2,1)}, f32[4,2,4,512]{3,2,1,0:T(4,128)S(1)}, bf16[4,1024,768]{1,2,0:T(8,128)(2,1)}, s32[]{:T(128)}, /*index=5*/s32[]{:T(128)}, s32[]{:T(128)}) while((s32[]{:T(128)}, bf16[4,1024,256]{2,1,0:T(8,128)(2,1)}, f32[4,2,4,512]{3,2,1,0:T(4,128)S(1)}, bf16[4,1024,768]{1,2,0:T(8,128)(2,1)}, ...), condition=%wide.region_17.18_spmd, body=%wide.region_12.17_spmd.sunk | while | flops 553777152 | bytes 37323008 | solution.py:127
  232.8 14.2 %while.76 = (s32[]{:T(128)}, bf16[2,512,256]{2,1,0:T(8,128)(2,1)}, f32[2,4,512]{2,1,0:T(4,128)S(1)}, bf16[2,512,4,64]{1,3,2,0:T(8,128)(2,1)}, bf16[1024,4,64]{0,...) while((s32[]{:T(128)}, bf16[2,512,256]{2,1,0:T(8,128)(2,1)}, f32[2,4,512]{2,1,0:T(4,128)S(1)}, ...), condition=%wide.region_16.16_spmd, body=%wide.region_13.15_spmd.sunk | while | flops 553777152 | bytes 27852896 | solution.py:56
  253.8 14.2 %while.76 = (s32[]{:T(128)}, bf16[2,512,256]{2,1,0:T(8,128)(2,1)}, f32[2,4,512]{2,1,0:T(4,128)S(1)}, bf16[2,512,4,64]{1,3,2,0:T(8,128)(2,1)}, bf16[1024,4,64]{0,...) while((s32[]{:T(128)}, bf16[2,512,256]{2,1,0:T(8,128)(2,1)}, f32[2,4,512]{2,1,0:T(4,128)S(1)}, ...), condition=%wide.region_16.16_spmd, body=%wide.region_13.15_spmd.sunk | while | flops 553777152 | bytes 27852896 | solution.py:56
  274.8 14.2 %while.76 = (s32[]{:T(128)}, bf16[2,512,256]{2,1,0:T(8,128)(2,1)}, f32[2,4,512]{2,1,0:T(4,128)S(1)}, bf16[2,512,4,64]{1,3,2,0:T(8,128)(2,1)}, bf16[1024,4,64]{0,...) while((s32[]{:T(128)}, bf16[2,512,256]{2,1,0:T(8,128)(2,1)}, f32[2,4,512]{2,1,0:T(4,128)S(1)}, ...), condition=%wide.region_16.16_spmd, body=%wide.region_13.15_spmd.sunk | while | flops 553777152 | bytes 27852896 | solution.py:56
  295.8 14.2 %while.76 = (s32[]{:T(128)}, bf16[2,512,256]{2,1,0:T(8,128)(2,1)}, f32[2,4,512]{2,1,0:T(4,128)S(1)}, bf16[2,512,4,64]{1,3,2,0:T(8,128)(2,1)}, bf16[1024,4,64]{0,...) while((s32[]{:T(128)}, bf16[2,512,256]{2,1,0:T(8,128)(2,1)}, f32[2,4,512]{2,1,0:T(4,128)S(1)}, ...), condition=%wide.region_16.16_spmd, body=%wide.region_13.15_spmd.sunk | while | flops 553777152 | bytes 27852896 | solution.py:56
  337.7 27.6 %fusion.50 = (bf16[1024,4096]{1,0:T(8,128)(2,1)}, f32[1024,4096]{1,0:T(8,128)}) fusion(f32[1024,4096]{1,0:T(8,128)} %fusion.85, bf16[1024,1024]{1,0:T(8,128)(2,1)} %bitcast.274, bf16[1024,4096]{1,0:T(8,128)(2,1)} %param.28), kind=kOutput, calls=%fused_computation.82 | convolution fusion | flops 8673820672 | bytes 52428800 | tf_op jit(solution)/shard_map/dot_general | solution.py:138
  365.3 13.2 %fusion.66 = (f32[1024]{0:T(1024)S(1)}, f32[1024,1024]{1,0:T(8,128)S(1)}) fusion(f32[4,1024]{1,0:T(4,128)S(1)} %copy-done.19, bf16[1024,4096]{1,0:T(8,128)(2,1)} %get-tuple-element.358, bf16[1024,4096]{1,0:T(8,128)(2,1)} %param.28), kind=kOutput, calls=%fused_computation.104 | convolution fusion | flops 8592030720 | bytes 20992000 | tf_op jit(solution)/shard_map/dot_general | solution.py:160
  406.2 15.7 %all-to-all-done.2 = bf16[4,256,1024]{1,0,2:T(4,128)(2,1)S(1)} async-done(((bf16[4,256,1024]{1,0,2:T(4,128)(2,1)}), bf16[4,256,1024]{1,0,2:T(4,128)(2,1)S(1)}, u32[]{:S(2)}, u32[]{:S(2)}) %all-to-all-start.2) | async-done | bytes 2097184 | tf_op jit(solution)/shard_map/all_to_all | solution.py:173
  429.7 141.1 %while.74 = (s32[]{:T(128)}, bf16[4,1024,768]{1,2,0:T(8,128)(2,1)}, bf16[4,1024,768]{1,2,0:T(8,128)(2,1)}, bf16[4,1024,256]{1,2,0:T(8,128)(2,1)}, f32[4,2,4,512]...) while((s32[]{:T(128)}, bf16[4,1024,768]{1,2,0:T(8,128)(2,1)}, ...), condition=%wide.region_22.23_spmd, body=%wide.region_18.22_spmd.sunk | while | flops 1370880000 | bytes 104948192 | solution.py:174
  438.1 23.2 %while.77 = (s32[]{:T(128)}, f32[1024,4,64]{0,2,1:T(8,128)S(1)}, f32[1024,4,64]{0,2,1:T(8,128)S(1)}, bf16[2,512,4,64]{1,3,2,0:T(8,128)(2,1)}, bf16[2,512,4,64]{1...) while((s32[]{:T(128)}, f32[1024,4,64]{0,2,1:T(8,128)S(1)}, ...), condition=%wide.region_21.21_spmd.clone, body=%wide.region_19.20_spmd.clone.sunk | while | flops 1368782848 | bytes 78700808 | solution.py:100
  473.3 23.2 %while.77 = (s32[]{:T(128)}, f32[1024,4,64]{0,2,1:T(8,128)S(1)}, f32[1024,4,64]{0,2,1:T(8,128)S(1)}, bf16[2,512,4,64]{1,3,2,0:T(8,128)(2,1)}, bf16[2,512,4,64]{1...) while((s32[]{:T(128)}, f32[1024,4,64]{0,2,1:T(8,128)S(1)}, ...), condition=%wide.region_21.21_spmd.clone, body=%wide.region_19.20_spmd.clone.sunk | while | flops 1368782848 | bytes 78700808 | solution.py:100
  508.6 23.2 %while.77 = (s32[]{:T(128)}, f32[1024,4,64]{0,2,1:T(8,128)S(1)}, f32[1024,4,64]{0,2,1:T(8,128)S(1)}, bf16[2,512,4,64]{1,3,2,0:T(8,128)(2,1)}, bf16[2,512,4,64]{1...) while((s32[]{:T(128)}, f32[1024,4,64]{0,2,1:T(8,128)S(1)}, ...), condition=%wide.region_21.21_spmd.clone, body=%wide.region_19.20_spmd.clone.sunk | while | flops 1368782848 | bytes 78700808 | solution.py:100
  543.8 23.2 %while.77 = (s32[]{:T(128)}, f32[1024,4,64]{0,2,1:T(8,128)S(1)}, f32[1024,4,64]{0,2,1:T(8,128)S(1)}, bf16[2,512,4,64]{1,3,2,0:T(8,128)(2,1)}, bf16[2,512,4,64]{1...) while((s32[]{:T(128)}, f32[1024,4,64]{0,2,1:T(8,128)S(1)}, ...), condition=%wide.region_21.21_spmd.clone, body=%wide.region_19.20_spmd.clone.sunk | while | flops 1368782848 | bytes 78700808 | solution.py:100
  581.5 76.8 %all_to_all.86 = bf16[4,1024,768]{2,0,1:T(4,128)(2,1)} all-to-all(bf16[4,1024,768]{2,0,1:T(4,128)(2,1)} %copy.52), channel_id=1, replica_groups=mesh['seq'=4,'batch'=8] {'seq'}, dimensions={1} | all-to-all | bytes 12582912 | tf_op jit(solution)/shard_map/all_to_all | solution.py:178
  683.8 18.6 %fusion.81 = f32[4096,1024]{1,0:T(8,128)} fusion(bf16[1024,1024]{1,0:T(8,128)(2,1)S(1)} %bitcast.273, f32[1024,4096]{1,0:T(8,128)} %get-tuple-element.359), kind=kOutput, calls=%fused_computation.139 | convolution fusion | flops 8627683328 | bytes 35651584 | tf_op jit(solution)/shard_map/dot_general | solution.py:24
  704.0 14.6 %fusion.88 = f32[1024,4096]{1,0:T(8,128)} fusion(bf16[1024,1024]{1,0:T(8,128)(2,1)S(1)} %bitcast.275, bf16[1024,4096]{1,0:T(8,128)(2,1)} %get-tuple-element.358), kind=kOutput, calls=%fused_computation.146 | convolution fusion | flops 8589934592 | bytes 27262976 | tf_op jit(solution)/shard_map/dot_general | solution.py:24
  720.5 12.2 dot_general.91
  732.7 12.8 fusion.64
  748.4 63.0 %reduce-scatter.7.cloned.1.call-done = f32[128,3072]{1,0:T(8,128)} async-done(((f32[1024,3072]{1,0:T(8,128)}), f32[128,3072]{1,0:T(8,128)}) %reduce-scatter.7.cloned.1.call-update) | async-done | bytes 1572880 | tf_op jit(solution)/shard_map/reduce_scatter | solution.py:191
  813.8 166.6 %reduce-scatter.13.cloned.1.call-done = f32[512,1024]{1,0:T(8,128)} async-done(((f32[4096,1024]{1,0:T(8,128)}), f32[512,1024]{1,0:T(8,128)}) %reduce-scatter.13.cloned.1.call-update) | async-done | bytes 2097168 | tf_op jit(solution)/shard_map/reduce_scatter | solution.py:194
  983.1 166.1 %reduce-scatter.11.cloned.1.call-done = f32[128,4096]{1,0:T(8,128)} async-done(((f32[1024,4096]{1,0:T(8,128)}), f32[128,4096]{1,0:T(8,128)}) %reduce-scatter.11.cloned.1.call-update) | async-done | bytes 2097168 | tf_op jit(solution)/shard_map/reduce_scatter | solution.py:193
  1152.0 17.4 %fusion.82 = f32[1024,1024]{1,0:T(8,128)} fusion(bf16[4096,1024]{1,0:T(8,128)(2,1)} %param.29, f32[1024,4096]{1,0:T(8,128)} %get-tuple-element.359), kind=kOutput, calls=%fused_computation.140 | convolution fusion | flops 8627683328 | bytes 29360128 | tf_op jit(solution)/shard_map/dot_general | solution.py:146
  1191.4 20.1 %reduce-scatter.15.cloned.1.call-done = f32[8,1024]{1,0:T(8,128)} async-done(((f32[64,1024]{1,0:T(8,128)}), f32[8,1024]{1,0:T(8,128)}) %reduce-scatter.15.cloned.1.call-update) | async-done | bytes 32784 | tf_op jit(solution)/shard_map/reduce_scatter | solution.py:195
  1212.2 16.8 %all-reduce = (bf16[8,1024]{1,0:T(8,128)(2,1)S(1)}, bf16[8,1024]{1,0:T(8,128)(2,1)S(1)}) all-reduce(bf16[8,1024]{1,0:T(8,128)(2,1)S(1)} %convert_element_type.136, bf16[8,1024]{1,0:T(8,128)(2,1)S(1)} %convert_element_type.138), channel_id=1, replica_groups=mesh['seq'=4,'batch'=8] {'seq'}, use_global_device_ids=true, to_apply=%region_35.36 | all-reduce | flops 16384 | bytes 65536 | tf_op jit(solution)/shard_map/psum | solution.py:203
  1230.3 71.3 %all-reduce.4.cloned.1.call-done = (bf16[128,3072]{1,0:T(8,128)(2,1)}, bf16[128,1024]{1,0:T(8,128)(2,1)}, bf16[128,4096]{1,0:T(8,128)(2,1)}, bf16[512,1024]{1,0:T(8,128)(2,1)}) async-done(((bf16[128,3072]{1,0:T(8,128)(2,1)}, bf16[128,1024]{1,0:T(8,128)(2,1)}, bf16[128,4096]{1,0:T(8,128)(2,1)}, bf16[512,1024]{1,0:T(8,128)(2,1)}), (bf16[128,3072]{1,0:T(8,128)(2,1)}, bf16[128,1024]{1,0:T(8,128)(2,1)}, ...) | async-done | bytes 3145744 | tf_op jit(solution)/shard_map/psum | solution.py:199
  (502 shorter events, 521.0 us)
Async XLA Ops:
  7.2 322.8 %copy-start = (bf16[1024,1024]{1,0:T(8,128)(2,1)S(1)}, bf16[1024,1024]{1,0:T(8,128)(2,1)}, u32[]{:S(2)}) copy-start(bf16[1024,1024]{1,0:T(8,128)(2,1)} %param.27) | copy-start | bytes 6291460
  7.2 5.5 copy-start.7
  7.2 6.6 copy-start.44
  13.8 8.6 copy-start.13
  33.1 6.3 copy-start.22
  33.1 77.0 %all-to-all-start = ((bf16[4,256,3072]{1,0,2:T(4,128)(2,1)}), bf16[4,256,3072]{1,0,2:T(4,128)(2,1)}, u32[]{:S(2)}, u32[]{:S(2)}) async-start(bf16[4,256,3072]{1,0,2:T(4,128)(2,1)} %copy.46), calls=%async_computation | async-start | bytes 12582912 | tf_op jit(solution)/shard_map/all_to_all | solution.py:126
  221.8 6.1 copy-start.29
  221.8 94.7 %all-to-all-start.1 = ((bf16[4,1024,256]{2,0,1:T(4,128)(2,1)}), bf16[4,1024,256]{2,0,1:T(4,128)(2,1)}, u32[]{:S(2)}, u32[]{:S(2)}) async-start(bf16[4,1024,256]{2,0,1:T(4,128)(2,1)} %copy.48), calls=%async_computation.1 | async-start | bytes 4194304 | tf_op jit(solution)/shard_map/all_to_all | solution.py:130
  316.5 77.2 %all-to-all-start.4 = ((bf16[4,1024,256]{2,0,1:T(4,128)(2,1)}), bf16[4,1024,256]{2,0,1:T(4,128)(2,1)}, u32[]{:S(2)}, u32[]{:S(2)}) async-start(bf16[4,1024,256]{2,0,1:T(4,128)(2,1)} %copy.54), calls=%async_computation.5 | async-start | bytes 4194304 | tf_op jit(solution)/shard_map/all_to_all | solution.py:130
  334.6 46.3 %copy-start.23 = (f32[4,256]{1,0:T(4,128)}, f32[4,256]{1,0:T(4,128)S(1)}, u32[]{:S(2)}) copy-start(f32[4,256]{1,0:T(4,128)S(1)} %broadcast_multiply_fusion.4) | copy-start | bytes 12292
  335.3 45.6 %copy-start.27 = (f32[4,256]{1,0:T(4,128)}, f32[4,256]{1,0:T(4,128)S(1)}, u32[]{:S(2)}) copy-start(f32[4,256]{1,0:T(4,128)S(1)} %add_rsqrt_fusion) | copy-start | bytes 12292
  365.3 13.2 %copy-start.5 = (f32[4,256,1024]{2,1,0:T(8,128)S(1)}, f32[4,256,1024]{2,1,0:T(8,128)}, u32[]{:S(2)}) copy-start(f32[4,256,1024]{2,1,0:T(8,128)} %copy-done.4) | copy-start | bytes 12582916
  393.7 28.2 %all-to-all-start.2 = ((bf16[4,256,1024]{1,0,2:T(4,128)(2,1)}), bf16[4,256,1024]{1,0,2:T(4,128)(2,1)S(1)}, u32[]{:S(2)}, u32[]{:S(2)}) async-start(bf16[4,256,1024]{1,0,2:T(4,128)(2,1)} %copy.50), calls=%async_computation.2 | async-start | bytes 4194304 | tf_op jit(solution)/shard_map/all_to_all | solution.py:173
  397.8 348.8 %reduce-scatter.9.cloned.1.call-start = ((), (), s32[]{:S(2)}) async-start(), calls=%async_computation.12 | async-start | bytes 4718592 | tf_op jit(solution)/shard_map/reduce_scatter | solution.py:192
  406.1 405.3 %reduce-scatter.7.cloned.1.call-start = ((), (), s32[]{:S(2)}) async-start(), calls=%async_computation.11 | async-start | bytes 14155776 | tf_op jit(solution)/shard_map/reduce_scatter | solution.py:191
  682.2 298.2 %reduce-scatter.13.cloned.1.call-start = ((), (), s32[]{:S(2)}) async-start(), calls=%async_computation.14 | async-start | bytes 18874368 | tf_op jit(solution)/shard_map/reduce_scatter | solution.py:194
  702.5 446.8 %reduce-scatter.11.cloned.1.call-start = ((), (), s32[]{:S(2)}) async-start(), calls=%async_computation.13 | async-start | bytes 18874368 | tf_op jit(solution)/shard_map/reduce_scatter | solution.py:193
  718.6 462.0 %reduce-scatter.17.cloned.1.call-start = ((), (), s32[]{:S(2)}) async-start(), calls=%async_computation.16 | async-start | bytes 294912 | tf_op jit(solution)/shard_map/reduce_scatter | solution.py:196
  720.4 491.0 %reduce-scatter.15.cloned.1.call-start = ((), (), s32[]{:S(2)}) async-start(), calls=%async_computation.15 | async-start | bytes 294912 | tf_op jit(solution)/shard_map/reduce_scatter | solution.py:195
  720.5 12.2 copy-start.8
  720.5 12.2 copy-start.26
  720.5 12.2 copy-start.32
  720.5 12.2 copy-start.38
  746.6 555.0 %all-reduce.4.cloned.1.call-start = ((), (), s32[]{:S(2)}) async-start(), calls=%async_computation.17 | async-start | bytes 6291456 | tf_op jit(solution)/shard_map/psum | solution.py:199
  1151.9 29.5 %copy-start.20 = (f32[4,1024]{1,0:T(4,128)S(1)}, f32[4,1024]{1,0:T(4,128)}, u32[]{:S(2)}) copy-start(f32[4,1024]{1,0:T(4,128)} %fusion.74) | copy-start | bytes 49156
  1151.9 29.5 %copy-start.24 = (f32[4,256]{1,0:T(4,128)S(1)}, f32[4,256]{1,0:T(4,128)}, u32[]{:S(2)}) copy-start(f32[4,256]{1,0:T(4,128)} %copy-done.23) | copy-start | bytes 12292
  1152.0 29.5 %copy-start.28 = (f32[4,256]{1,0:T(4,128)S(1)}, f32[4,256]{1,0:T(4,128)}, u32[]{:S(2)}) copy-start(f32[4,256]{1,0:T(4,128)} %copy-done.27) | copy-start | bytes 12292
  1152.0 29.5 %copy-start.34 = (f32[4,256]{1,0:T(4,128)S(1)}, f32[4,256]{1,0:T(4,128)}, u32[]{:S(2)}) copy-start(f32[4,256]{1,0:T(4,128)} %copy-done.33) | copy-start | bytes 12292
  1152.0 29.5 %copy-start.36 = (f32[4,256]{1,0:T(4,128)S(1)}, f32[4,256]{1,0:T(4,128)}, u32[]{:S(2)}) copy-start(f32[4,256]{1,0:T(4,128)} %copy-done.35) | copy-start | bytes 12292
  1152.0 29.5 %copy-start.43 = (f32[4]{0:T(128)S(1)}, f32[4]{0:T(128)}, u32[]{:S(2)}) copy-start(f32[4]{0:T(128)} %copy-done.41) | copy-start | bytes 52
  1301.5 7.2 copy-start.18
  1303.4 6.9 copy-start.1
  (52 other events, 106.0 us)
Sparse Core Ops, SparseCore 0:
  406.3 51.9 reduce-scatter.8
  682.4 128.9 reduce-scatter.6
  813.8 166.5 reduce-scatter.12
  982.6 166.5 reduce-scatter.10
  1151.9 28.7 reduce-scatter.16
  1182.8 28.5 reduce-scatter.14
  1215.4 86.0 all-reduce.3
where the time goes:
time: 1330 us; the launch traced here: 1320 us
  waiting for transfers between devices  566 us (43%)
  matrix products  298 us (22%)
  local copies, waits for them, and re-layouts  227 us (17%)
  other arithmetic  96.7 us (7%)
  blocking collectives  93.5 us (7%)
  starting transfers between devices  19.1 us (1%)
  between operations  15.8 us (1%)
    reduce_scatter x1, waiting for transfers between devices, body(): lax.psum_scatter(gradients[3], 'batch', scatter_dimension=0, tiled=True)  167 us
    reduce_scatter x1, waiting for transfers between devices, body(): lax.psum_scatter(gradients[2], 'batch', scatter_dimension=0, tiled=True)  166 us
    all_to_all x1, blocking collectives, body(): lax.all_to_all(grad_packed_heads, 'seq', split_axis=1, concat_axis=2, til...  76.8 us
    psum x1, waiting for transfers between devices, body(): lax.psum(shares[0].astype(jnp.bfloat16), 'seq').astype(jnp.float32)  71.3 us
    reduce_scatter x1, waiting for transfers between devices, body(): lax.psum_scatter(gradients[0], 'batch', scatter_dimension=0, tiled=True)  63 us
    dot_general x24, matrix products, per_block(): jnp.einsum('qhd,khd->hqk', query_block, key_rows, preferred_element_type=...  58 us
    all_to_all x1, waiting for transfers between devices, attention_part(): lax.all_to_all(packed, 'seq', split_axis=2, concat_axis=1, tiled=True)  51.6 us
    dot_general x4, matrix products, weight_grad(): lax.dot_general(left, right, (((0,), (0,)), ((), ())), preferred_element_...  46.8 us
  transfers between devices with their start and end apart: 11, of which 8 were waited for; matrix products, arithmetic and copies ran while one was open for 35% of the time, Pallas kernels for 0%

commit v1 on v0

v1 whole, which is shorter than its diff:
```python
import functools
import math

import jax
import jax.numpy as jnp
from jax import lax
from jax.experimental import pallas as pl
from jax.experimental.pallas import tpu as pltpu
from jax.sharding import PartitionSpec as P

F32 = jnp.float32
BF16 = jnp.bfloat16
HEAD = 64
LOG2E = math.log2(math.e)
GELU_C = math.sqrt(2 / math.pi)
GELU_K = 0.044715
VMEM = 60 * 2**20


def dot(a, b, ca, cb):
    return lax.dot_general(a, b, (((ca,), (cb,)), ((), ())), preferred_element_type=F32)


def nn(a, b):
    return dot(a, b, 1, 0)


def nt(a, b):
    return dot(a, b, 1, 1)


def tn(a, b):
    return dot(a, b, 0, 0)


def whole(shape):
    zeros = (0,) * len(shape)
    return pl.BlockSpec(shape, lambda i: zeros, pipeline_mode=pl.Buffered(1))


def params():
    return pltpu.CompilerParams(vmem_limit_bytes=VMEM)


def norm_rows(v):
    centred = v - jnp.mean(v, axis=-1, keepdims=True)
    inverse = lax.rsqrt(jnp.mean(centred * centred, axis=-1, keepdims=True) + 1e-05)
    return centred * inverse, inverse


def norm_back(g, normed, inverse):
    first = jnp.mean(g, axis=-1, keepdims=True)
    second = jnp.mean(g * normed, axis=-1, keepdims=True)
    return inverse * (g - first - normed * second)


def qkv_kernel(pieces, *refs):
    toks, (gain, w, x_out, ready_out, packed) = refs[:pieces], refs[pieces:]
    rows = toks[0].shape[0]

    @pl.when(pl.program_id(0) == 0)
    def _():
        for k in range(pieces):
            span = slice(k * rows, (k + 1) * rows)
            t = toks[k][...]
            x_out[span] = t
            ready_out[span] = (norm_rows(t.astype(F32))[0] * gain[...]).astype(BF16)

    packed[...] = nn(ready_out[...], w[...]).astype(BF16)


def qkv(toks, gain, w):
    rows, width = toks[0].shape
    length = rows * len(toks)
    cols = w.shape[1]
    block = min(1024, cols)
    return pl.pallas_call(
        functools.partial(qkv_kernel, len(toks)),
        grid=(cols // block,),
        in_specs=[whole((rows, width))] * len(toks)
        + [whole((1, width)), pl.BlockSpec((width, block), lambda i: (0, i))],
        out_specs=[
            whole((length, width)),
            whole((length, width)),
            pl.BlockSpec((length, block), lambda i: (0, i)),
        ],
        out_shape=[
            jax.ShapeDtypeStruct((length, width), BF16),
            jax.ShapeDtypeStruct((length, width), BF16),
            jax.ShapeDtypeStruct((length, cols), BF16),
        ],
        compiler_params=params(),
        name="norm_qkv",
    )(*toks, gain, w)


def split2(v):
    hi = v.astype(BF16)
    return hi, (v - hi.astype(F32)).astype(BF16)


def split3(v):
    a = v.astype(BF16).astype(F32)
    b = (v - a).astype(BF16).astype(F32)
    return a, b, v - a - b


def in_lanes(columns, first, rows):
    lane = lax.broadcasted_iota(jnp.int32, (rows, 128), 1)
    out = jnp.zeros((rows, 128), F32)
    for i, column in enumerate(columns):
        out = jnp.where(lane == first + i, column, out)
    return out.astype(BF16)


def lanes_between(rows, low, high):
    lane = lax.broadcasted_iota(jnp.int32, (rows, 128), 1)
    return ((lane >= low) & (lane < high)).astype(F32).astype(BF16)


def head_parts(p, h):
    base = 3 * HEAD * h
    return p[:, base : base + HEAD], p[:, base + HEAD : base + 2 * HEAD], p[:, base + 2 * HEAD : base + 3 * HEAD]


def attend_kernel(p_ref, o_ref, aux_ref, *, bq):
    length = p_ref.shape[0]

    def run(exact):
        mixed, auxes, low, high = [], [], [], []
        for h in range(2):
            q, k, v = head_parts(p_ref, h)
            scaled = q.astype(F32) * (LOG2E * HEAD**-0.5)
            qhi, qlo = split2(scaled)
            vv = jnp.concatenate([v, jnp.ones((length, HEAD), BF16)], axis=1)
            if exact:
                qq = jnp.concatenate([qhi, qlo], axis=1)
                kk = jnp.concatenate([k, k], axis=1)
            else:
                k32 = k.astype(F32)
                knorm = jnp.sqrt(jnp.max(jnp.sum(k32 * k32, axis=1, keepdims=True)))
                bound = jnp.sqrt(jnp.sum(scaled * scaled, axis=1, keepdims=True)) * knorm
                b1 = bound.astype(BF16).astype(F32)
                qq = jnp.concatenate([qhi, qlo, in_lanes([-b1], 0, length)], axis=1)
                kk = jnp.concatenate([k, k, lanes_between(length, 0, 1)], axis=1)
            parts, aux = [], []
            for i in range(length // bq):
                span = slice(i * bq, (i + 1) * bq)
                s = nt(qq[span], kk)
                if exact:
                    m = jnp.max(s, axis=1, keepdims=True)
                    s = s - m
                else:
                    m = b1[span]
                o = nn(jnp.exp2(s).astype(BF16), vv)
                total = o[:, HEAD : HEAD + 1]
                parts.append((o[:, :HEAD] * (1.0 / total)).astype(BF16))
                aux.append(in_lanes(split3(-(m + jnp.log2(total))), 4 * h, bq))
                low.append(jnp.min(total))
                high.append(jnp.max(total))
            mixed.append(jnp.concatenate(parts, axis=0))
            auxes.append(jnp.concatenate(aux, axis=0))
        o_ref[...] = jnp.concatenate(mixed, axis=1)
        aux_ref[...] = auxes[0] + auxes[1]
        return functools.reduce(jnp.minimum, low), functools.reduce(jnp.maximum, high)

    low, high = run(False)
    fine = (low > 2.0**-80) & (high < 2.0**80)

    @pl.when(jnp.logical_not(fine))
    def _():
        run(True)


def attend(packed):
    length, cols = packed.shape
    pairs = cols // (6 * HEAD)
    out = pl.BlockSpec((length, 2 * HEAD), lambda i: (0, i))
    shape = jax.ShapeDtypeStruct((length, pairs * 2 * HEAD), BF16)
    return pl.pallas_call(
        functools.partial(attend_kernel, bq=math.gcd(length, 256)),
        grid=(pairs,),
        in_specs=[pl.BlockSpec((length, 6 * HEAD), lambda i: (0, i))],
        out_specs=[out, out],
        out_shape=[shape, shape],
        compiler_params=params(),
        name="attend",
    )(packed)


def attend_back_math(p_ref, o_ref, aux_ref, do_ref, bq):
    length = p_ref.shape[0]
    aux = aux_ref[...]
    outs = []
    for h in range(2):
        q, k, v = head_parts(p_ref, h)
        do = do_ref[:, HEAD * h : HEAD * (h + 1)]
        o = o_ref[:, HEAD * h : HEAD * (h + 1)]
        qhi, qlo = split2(q.astype(F32) * (LOG2E * HEAD**-0.5))
        qq = jnp.concatenate([qhi, qlo, aux], axis=1)
        kk = jnp.concatenate([k, k, lanes_between(length, 4 * h, 4 * h + 3)], axis=1)
        minus = -jnp.sum(do.astype(F32) * o.astype(F32), axis=1, keepdims=True)
        dd = jnp.concatenate([do, in_lanes(split3(minus), 0, length)[:, :HEAD]], axis=1)
        vv = jnp.concatenate([v, lanes_between(length, 0, 3)[:, :HEAD]], axis=1)
        do_t, q_t = do.T, q.T
        dv_t = jnp.zeros((HEAD, length), F32)
        dk_t = jnp.zeros((HEAD, length), F32)
        dq = []
        for i in range(length // bq):
            span = slice(i * bq, (i + 1) * bq)
            p = jnp.exp2(nt(qq[span], kk))
            ds = (p * nt(dd[span], vv)).astype(BF16)
            dv_t = dv_t + nn(do_t[:, span], p.astype(BF16))
            dk_t = dk_t + nn(q_t[:, span], ds)
            dq.append((nn(ds, k) * HEAD**-0.5).astype(BF16))
        outs += [
            jnp.concatenate(dq, axis=0),
            (dk_t * HEAD**-0.5).astype(BF16).T,
            dv_t.astype(BF16).T,
        ]
    return jnp.concatenate(outs, axis=1)


def mlp_kernel(pieces, *refs):
    x, mixed, w_out, gain, alive = refs[:5]
    cots = refs[5 : 5 + pieces]
    w_up, hidden, ready, gout, act, slope, grad_down = refs[5 + pieces :]
    rows = cots[0].shape[0]

    @pl.when(pl.program_id(0) == 0)
    def _():
        for k in range(pieces):
            span = slice(k * rows, (k + 1) * rows)
            gout[span] = cots[k][...] * alive[...].astype(BF16)
            h = x[span].astype(F32) + nn(mixed[span], w_out[...])
            hidden[span] = h
            ready[span] = (norm_rows(h)[0] * gain[...]).astype(BF16)

    u = nn(ready[...], w_up[...])
    u2 = u * u
    t = jnp.tanh(u * (GELU_C + (GELU_C * GELU_K) * u2))
    half = 0.5 + 0.5 * t
    a = (u * half).astype(BF16)
    act[...] = a
    slope[...] = (half + u * (1 - t * t) * (0.5 * GELU_C + (1.5 * GELU_C * GELU_K) * u2)).astype(BF16)
    grad_down[...] = tn(a, gout[...]).astype(BF16)


def mlp(x, mixed, w_out, gain, alive, cots, w_up):
    length, width = x.shape
    inner = w_up.shape[1]
    rows = length // len(cots)
    block = min(1024, inner)
    cols = pl.BlockSpec((length, block), lambda i: (0, i))
    return pl.pallas_call(
        functools.partial(mlp_kernel, len(cots)),
        grid=(inner // block,),
        in_specs=[
            whole((length, width)),
            whole((length, width)),
            whole((width, width)),
            whole((1, width)),
            whole((1, width)),
        ]
        + [whole((rows, width))] * len(cots)
        + [pl.BlockSpec((width, block), lambda i: (0, i))],
        out_specs=[whole((length, width))] * 3 + [cols, cols, pl.BlockSpec((block, width), lambda i: (i, 0))],
        out_shape=[
            jax.ShapeDtypeStruct((length, width), F32),
            jax.ShapeDtypeStruct((length, width), BF16),
            jax.ShapeDtypeStruct((length, width), BF16),
            jax.ShapeDtypeStruct((length, inner), BF16),
            jax.ShapeDtypeStruct((length, inner), BF16),
            jax.ShapeDtypeStruct((inner, width), BF16),
        ],
        compiler_params=params(),
        name="mlp",
    )(x, mixed, w_out, gain, alive, *cots, w_up)


def mlp_back_kernel(
    gout, act, slope, w_down, w_up, ready, hidden, gain, mixed, w_out,
    out, grad_up, grad_hidden, grad_out, grad_mixed, table, out_sum, back_sum,
):
    i = pl.program_id(0)

    @pl.when(i == 0)
    def _():
        out_sum[...] = hidden[...]
        back_sum[...] = jnp.zeros_like(back_sum)

    gu = (nt(gout[...], w_down[...]) * slope[...].astype(F32)).astype(BF16)
    grad_up[...] = tn(ready[...], gu).astype(BF16)
    back_sum[...] += nt(gu, w_up[...])
    out_sum[...] += nn(act[...], w_down[...])

    @pl.when(i == pl.num_programs(0) - 1)
    def _():
        length = gout.shape[0]
        step = math.gcd(length, 256)
        total = jnp.zeros((1, gain.shape[1]), F32)
        for r in range(length // step):
            span = slice(r * step, (r + 1) * step)
            normed, inverse = norm_rows(hidden[span])
            g = back_sum[span]
            total = total + jnp.sum(g * normed, axis=0, keepdims=True)
            grad_hidden[span] = gout[span].astype(F32) + norm_back(g * gain[...], normed, inverse)
            out[span] = out_sum[span].astype(BF16)
        table[...] = total
        low = grad_hidden[...].astype(BF16)
        grad_mixed[...] = nt(low, w_out[...]).astype(BF16)
        grad_out[...] = tn(mixed[...], low).astype(BF16)


def mlp_back(gout, act, slope, w_down, w_up, ready, hidden, gain, mixed, w_out):
    length, width = gout.shape
    inner = w_up.shape[1]
    block = min(1024, inner)
    cols = pl.BlockSpec((length, block), lambda i: (0, i))
    square = whole((length, width))
    return pl.pallas_call(
        mlp_back_kernel,
        grid=(inner // block,),
        in_specs=[
            square,
            cols,
            cols,
            pl.BlockSpec((block, width), lambda i: (i, 0)),
            pl.BlockSpec((width, block), lambda i: (0, i)),
            square,
            square,
            whole((1, width)),
            square,
            whole((width, width)),
        ],
        out_specs=[
            square,
            pl.BlockSpec((width, block), lambda i: (0, i)),
            square,
            whole((width, width)),
            square,
            whole((1, width)),
        ],
        out_shape=[
            jax.ShapeDtypeStruct((length, width), BF16),
            jax.ShapeDtypeStruct((width, inner), BF16),
            jax.ShapeDtypeStruct((length, width), F32),
            jax.ShapeDtypeStruct((width, width), BF16),
            jax.ShapeDtypeStruct((length, width), BF16),
            jax.ShapeDtypeStruct((1, width), F32),
        ],
        scratch_shapes=[pltpu.VMEM((length, width), F32)] * 2,
        compiler_params=params(),
        name="mlp_back",
    )(gout, act, slope, w_down, w_up, ready, hidden, gain, mixed, w_out)


def attn_back_kernel(
    packed, mixed, aux, grad_mixed, w_qkv, ready, x, grad_hidden, gain,
    grad_qkv, grad_x, table, back_sum, *, bq,
):
    i = pl.program_id(0)

    @pl.when(i == 0)
    def _():
        back_sum[...] = jnp.zeros_like(back_sum)

    gp = attend_back_math(packed, mixed, aux, grad_mixed, bq)
    grad_qkv[...] = tn(ready[...], gp).astype(BF16)
    back_sum[...] += nt(gp, w_qkv[...])

    @pl.when(i == pl.num_programs(0) - 1)
    def _():
        length = x.shape[0]
        step = math.gcd(length, 256)
        total = jnp.zeros((1, gain.shape[1]), F32)
        for r in range(length // step):
            span = slice(r * step, (r + 1) * step)
            normed, inverse = norm_rows(x[span].astype(F32))
            g = back_sum[span]
            total = total + jnp.sum(g * normed, axis=0, keepdims=True)
            grad_x[span] = (grad_hidden[span] + norm_back(g * gain[...], normed, inverse)).astype(BF16)
        table[...] = total


def attn_back(packed, mixed, aux, grad_mixed, w_qkv, ready, x, grad_hidden, gain):
    length, width = x.shape
    cols = packed.shape[1]
    pairs = cols // (6 * HEAD)
    pair = pl.BlockSpec((length, 2 * HEAD), lambda i: (0, i))
    square = whole((length, width))
    return pl.pallas_call(
        functools.partial(attn_back_kernel, bq=math.gcd(length, 256)),
        grid=(pairs,),
        in_specs=[
            pl.BlockSpec((length, 6 * HEAD), lambda i: (0, i)),
            pair,
            pair,
            pair,
            pl.BlockSpec((width, 6 * HEAD), lambda i: (0, i)),
            square,
            square,
            square,
            whole((1, width)),
        ],
        out_specs=[
            pl.BlockSpec((width, 6 * HEAD), lambda i: (0, i)),
            square,
            whole((1, width)),
        ],
        out_shape=[
            jax.ShapeDtypeStruct((width, cols), BF16),
            jax.ShapeDtypeStruct((length, width), BF16),
            jax.ShapeDtypeStruct((1, width), F32),
        ],
        scratch_shapes=[pltpu.VMEM((length, width), F32)],
        compiler_params=params(),
        name="attn_back",
    )(packed, mixed, aux, grad_mixed, w_qkv, ready, x, grad_hidden, gain)


def exchange(pieces, me, ways):
    return [pieces[0]] + [
        lax.ppermute(pieces[k], "seq", [(s, s ^ k) for s in range(ways)]) for k in range(1, ways)
    ]


def by_partner(slots, me, ways):
    return [lax.dynamic_index_in_dim(slots, me ^ k, 0, keepdims=False) for k in range(ways)]


def to_slots(pieces, me, ways):
    stacked = jnp.stack(pieces)
    return jnp.take(stacked, jnp.arange(ways) ^ me, axis=0)


def body(tokens, cotangent, bins, live_count, w_qkv, w_out, w_up, w_down, gain_attn, gain_mlp):
    slots, rows, width = tokens.shape
    ways = lax.axis_size("seq")
    me = lax.axis_index("seq")
    toks = exchange(by_partner(tokens, me, ways), me, ways)
    cots = exchange(by_partner(cotangent, me, ways), me, ways)
    my_bin = lax.dynamic_index_in_dim(bins, me, 0)
    row_attn = lax.dynamic_slice_in_dim(gain_attn, my_bin[0], 1, 0)
    row_mlp = lax.dynamic_slice_in_dim(gain_mlp, my_bin[0], 1, 0)
    alive = jnp.broadcast_to((me < live_count[0]).astype(F32), (1, width))

    x, ready_attn, packed = qkv(toks, row_attn, w_qkv)
    mixed, aux = attend(packed)
    hidden, ready_mlp, gout, act, slope, grad_down = mlp(x, mixed, w_out, row_mlp, alive, cots, w_up)
    out, grad_up, grad_hidden, grad_out, grad_mixed, sum_mlp = mlp_back(
        gout, act, slope, w_down, w_up, ready_mlp, hidden, row_mlp, mixed, w_out
    )
    grad_qkv, grad_x, sum_attn = attn_back(
        packed, mixed, aux, grad_mixed, w_qkv, ready_attn, x, grad_hidden, row_attn
    )

    def back_to_slots(rows_out):
        parts = rows_out.reshape(ways, rows, width)
        return to_slots(exchange([parts[k] for k in range(ways)], me, ways), me, ways)

    output = back_to_slots(out)
    grad_tokens = back_to_slots(grad_x).astype(F32)
    onehot = (jnp.arange(gain_attn.shape[0], dtype=jnp.int32) == my_bin[0]).astype(F32)[:, None]

    def total(v, low):
        share = lax.psum_scatter(v, "batch", scatter_dimension=0, tiled=True)
        return lax.psum(share.astype(low), "seq").astype(F32)

    return (
        output,
        grad_tokens,
        total(grad_qkv, BF16),
        total(grad_out, BF16),
        total(grad_up, BF16),
        total(grad_down, BF16),
        total(onehot * sum_attn, F32),
        total(onehot * sum_mlp, F32),
    )


def solution(mesh):
    placed = (
        P("batch", "seq", None),
        P("batch", "seq", None),
        P("batch"),
        P("batch"),
        P(),
        P(),
        P(),
        P(),
        P(),
        P(),
    )
    return jax.shard_map(
        body,
        mesh=mesh,
        in_specs=placed,
        out_specs=(
            P("batch", "seq", None),
            P("batch", "seq", None),
            P("batch", None),
            P("batch", None),
            P("batch", None),
            P("batch", None),
            P("batch", None),
            P("batch", None),
        ),
        check_vma=False,
    )
```

time: 1330 us -> 708 us (0.53)
  matrix products: 298 us -> 0 us
  local copies, waits for them, and re-layouts: 227 us -> 15.1 us
  Pallas kernels: 0 us -> 203 us
  waiting for transfers between devices: 566 us -> 430 us
  blocking collectives: 93.5 us -> 0 us
  other arithmetic: 96.7 us -> 15.3 us
    dot_general x88 -> x0, matrix products: 298 us -> none  [the longest x24 58 us: per_block(): jnp.einsum('qhd,khd->hqk', query_block, key_rows, preferred_element_type=...]
    pallas_call x0 -> x5, Pallas kernels: none -> 203 us  [the longest x1 70.1 us: attn_back(): pl.pallas_call(functools.partial(attn_back_kernel, bq=math.gcd(length, 25...]
    reduce_scatter x6, waiting for transfers between devices: 427 us -> 259 us  [total(): share = lax.psum_scatter(v, 'batch', scatter_dimension=0, tiled=True)]
    all_to_all x1 -> x0, blocking collectives: 76.8 us -> none  [body(): lax.all_to_all(grad_packed_heads, 'seq', split_axis=1, concat_axis=2, til...]
    all_to_all x4 -> x0, waiting for transfers between devices: 67.3 us -> none  [the longest x1 51.6 us: attention_part(): lax.all_to_all(packed, 'seq', split_axis=2, concat_axis=1, tiled=True)]
    psum x1 -> x2, waiting for transfers between devices: 71.3 us -> 122 us  [total(): return lax.psum(share.astype(low), 'seq').astype(F32)]
    all_to_all x7 -> x0, local copies, waits for them, and re-layouts: 47.2 us -> none  [the longest x2 21.3 us: attention_part(): lax.all_to_all(packed, 'seq', split_axis=2, concat_axis=1, tiled=True)]
    ppermute x0 -> x12, waiting for transfers between devices: none -> 47.1 us  [exchange(): lax.ppermute(pieces[k], 'seq', [(s, s ^ k) for s in range(ways)])]
  transfers between devices with their start and end apart: 11 -> 20, of which waited for: 8 -> 13; matrix products, arithmetic and copies ran while one was open for 35% -> 3% of each run, Pallas kernels for 0% -> 16%
where the time goes in v1:
time: 708 us; the launch traced here: 699 us
  waiting for transfers between devices  430 us (61%)
  Pallas kernels  203 us (29%)
  starting transfers between devices  19.4 us (3%)
  between operations  17 us (2%)
  other arithmetic  15.3 us (2%)
  local copies, waits for them, and re-layouts  15.1 us (2%)
    reduce_scatter x6, waiting for transfers between devices, total(): share = lax.psum_scatter(v, 'batch', scatter_dimension=0, tiled=True)  259 us
    psum x2, waiting for transfers between devices, total(): return lax.psum(share.astype(low), 'seq').astype(F32)  122 us
    pallas_call x1, Pallas kernels, attn_back(): pl.pallas_call(functools.partial(attn_back_kernel, bq=math.gcd(length, 25...  70.1 us
    pallas_call x1, Pallas kernels, mlp_back(): pl.pallas_call(mlp_back_kernel, grid=(inner // block,), in_specs=[square,...  56.2 us
    ppermute x12, waiting for transfers between devices, exchange(): lax.ppermute(pieces[k], 'seq', [(s, s ^ k) for s in range(ways)])  47.1 us
    pallas_call x1, Pallas kernels, attend(): pl.pallas_call(functools.partial(attend_kernel, bq=math.gcd(length, 256))...  33 us
    pallas_call x1, Pallas kernels, mlp(): pl.pallas_call(functools.partial(mlp_kernel, len(cots)), grid=(inner // b...  31.4 us
    ppermute x12, starting transfers between devices, exchange(): lax.ppermute(pieces[k], 'seq', [(s, s ^ k) for s in range(ways)])  18.9 us
  transfers between devices with their start and end apart: 20, of which 13 were waited for; matrix products, arithmetic and copies ran while one was open for 3% of the time, Pallas kernels for 16%

profile of v1, /device:TPU:0, one launch (start us, length us, event | category | flops | bytes accessed | tf_op | source)
XLA Modules:
  0.0 699.1 jit_solution(8963148119521221284)
XLA Ops:
  7.3 2.7 dynamic-slice_bitcast_fusion.4
  10.0 2.9 collective-permute-start
  12.9 1.5 collective-permute-start.1
  15.5 2.0 collective-permute-start.3
  17.5 1.5 collective-permute-start.4
  19.0 6.7 collective-permute-done.refs_1_
  25.7 3.0 collective-permute-start.5
  33.7 5.4 collective-permute-done.1.refs_2_
  39.1 12.0 %norm_qkv.1 = (bf16[1024,1024]{1,0:T(8,128)(2,1)}, bf16[1024,1024]{1,0:T(8,128)(2,1)}, bf16[1024,3072]{1,0:T(8,128)(2,1)}) custom-call(bf16[256,1024]{1,0:T(8,128)(2,1)} %get-tuple-element.69.refs_0_, bf16[256,1024]{1,0:T(8,128)(2,1)} %copy-done.7, bf16[256,1024]{1,0:T(8,128)(2,1)} %collective-permute-done.1.refs_2_, ...), custom_call_target="tpu_custom_call" | custom-call | tf_op jit(solution)/shard_map/norm_qkv/pallas_call | solution.py:77
  51.1 33.0 %attend.1 = (bf16[1024,1024]{1,0:T(8,128)(2,1)}, bf16[1024,1024]{1,0:T(8,128)(2,1)}) custom-call(bf16[1024,3072]{1,0:T(8,128)(2,1)} %get-tuple-element.30.p_ref.packed), custom_call_target="tpu_custom_call" | custom-call | tf_op jit(solution)/shard_map/attend/pallas_call | solution.py:180
  84.6 31.4 %mlp.1 = (f32[1024,1024]{1,0:T(8,128)}, bf16[1024,1024]{1,0:T(8,128)(2,1)}, bf16[1024,1024]{1,0:T(8,128)(2,1)}, bf16[1024,4096]{1,0:T(8,128)(2,1)}, bf16[1024,40...) custom-call(bf16[1024,1024]{1,0:T(8,128)(2,1)} %get-tuple-element.29.refs_0_.x, ...), custom_call_target="tpu_custom_call" | custom-call | tf_op jit(solution)/shard_map/mlp/pallas_call | solution.py:255
  116.0 56.2 %mlp_back.1 = (bf16[1024,1024]{1,0:T(8,128)(2,1)}, bf16[1024,4096]{1,0:T(8,128)(2,1)}, f32[1024,1024]{1,0:T(8,128)}, bf16[1024,1024]{1,0:T(8,128)(2,1)}, bf16[1024,1024]{1,0:T(8,128)(2,1)}, /*index=5*/f32[1,1024]{1,0:T(1,128)}) custom-call(bf16[1024,1024]{1,0:T(8,128)(2,1)} %get-tuple-element.32.gout, bf16[1024,4096]{1,0:T(8,128)(2,1)} %get-tuple-element.33.act, ...), custom_call_target="tpu_custom_call" | custom-call | tf_op jit(solution)/shard_map/mlp_back/pallas_call | solution.py:321
  172.3 70.1 %attn_back.1 = (bf16[1024,3072]{1,0:T(8,128)(2,1)}, bf16[1024,1024]{1,0:T(8,128)(2,1)}, f32[1,1024]{1,0:T(1,128)}) custom-call(bf16[1024,3072]{1,0:T(8,128)(2,1)} %get-tuple-element.30.p_ref.packed, bf16[1024,1024]{1,0:T(8,128)(2,1)} %get-tuple-element.31.refs_1_.mixed, bf16[1024,1024]{1,0:T(8,128)(2,1)} %get-tuple-element.38.aux, ...), custom_call_target="tpu_custom_call" | custom-call | tf_op jit(solution)/shard_map/attn_back/pallas_call | solution.py:392
  246.0 66.7 %reduce-scatter.7.cloned.1.call-done = bf16[128,3072]{1,0:T(8,128)(2,1)} async-done(((bf16[1024,3072]{1,0:T(8,128)(2,1)}), bf16[128,3072]{1,0:T(8,128)(2,1)}) %reduce-scatter.7.cloned.1.call-update) | async-done | bytes 786448 | tf_op jit(solution)/shard_map/reduce_scatter | solution.py:467
  312.7 90.3 %reduce-scatter.11.cloned.1.call-done = bf16[128,4096]{1,0:T(8,128)(2,1)} async-done(((bf16[1024,4096]{1,0:T(8,128)(2,1)}), bf16[128,4096]{1,0:T(8,128)(2,1)}) %reduce-scatter.11.cloned.1.call-update) | async-done | bytes 1048592 | tf_op jit(solution)/shard_map/reduce_scatter | solution.py:467
  403.0 90.1 %reduce-scatter.13.cloned.1.call-done = bf16[512,1024]{1,0:T(8,128)(2,1)} async-done(((bf16[4096,1024]{1,0:T(8,128)(2,1)}), bf16[512,1024]{1,0:T(8,128)(2,1)}) %reduce-scatter.13.cloned.1.call-update) | async-done | bytes 1048592 | tf_op jit(solution)/shard_map/reduce_scatter | solution.py:467
  493.6 2.5 collective-permute-start.11
  498.3 2.4 collective-permute-start.8
  501.2 8.2 %collective-permute-done.11 = bf16[256,1024]{1,0:T(8,128)(2,1)S(1)} collective-permute-done((bf16[256,1024]{1,0:T(8,128)(2,1)S(1)}, bf16[256,1024]{1,0:T(8,128)(2,1)S(1)}, u32[]{:S(2)}, u32[]{:S(2)}) %collective-permute-start.11) | collective-permute-done | bytes 524320 | tf_op jit(solution)/shard_map/ppermute | solution.py:424
  510.9 9.8 %collective-permute-done.10 = bf16[256,1024]{1,0:T(8,128)(2,1)S(1)} collective-permute-done((bf16[256,1024]{1,0:T(8,128)(2,1)S(1)}, bf16[256,1024]{1,0:T(8,128)(2,1)S(1)}, u32[]{:S(2)}, u32[]{:S(2)}) %collective-permute-start.10) | collective-permute-done | bytes 524320 | tf_op jit(solution)/shard_map/ppermute | solution.py:424
  521.0 2.0 gather_fusion.1
  523.0 9.1 %collective-permute-done.8 = bf16[256,1024]{1,0:T(8,128)(2,1)} collective-permute-done((bf16[256,1024]{1,0:T(8,128)(2,1)}, bf16[256,1024]{1,0:T(8,128)(2,1)}, u32[]{:S(2)}, u32[]{:S(2)}) %collective-permute-start.8) | collective-permute-done | bytes 524320 | tf_op jit(solution)/shard_map/ppermute | solution.py:424
  532.0 7.8 %collective-permute-done.7 = bf16[256,1024]{1,0:T(8,128)(2,1)} collective-permute-done((bf16[256,1024]{1,0:T(8,128)(2,1)}, bf16[256,1024]{1,0:T(8,128)(2,1)}, u32[]{:S(2)}, u32[]{:S(2)}) %collective-permute-start.7) | collective-permute-done | bytes 524320 | tf_op jit(solution)/shard_map/ppermute | solution.py:424
  540.0 1.6 pad_maximum_fusion
  541.6 2.0 gather_fusion
  543.6 11.7 %reduce-scatter.17.cloned.1.call-done = f32[8,1024]{1,0:T(8,128)} async-done(((f32[64,1024]{1,0:T(8,128)}), f32[8,1024]{1,0:T(8,128)}) %reduce-scatter.17.cloned.1.call-update) | async-done | bytes 32784 | tf_op jit(solution)/shard_map/reduce_scatter | solution.py:467
  555.3 5.4 select_convert_fusion
  560.7 83.9 %all-reduce.7.cloned.1.call-done = (bf16[128,3072]{1,0:T(8,128)(2,1)}, bf16[128,1024]{1,0:T(8,128)(2,1)}, bf16[128,4096]{1,0:T(8,128)(2,1)}, bf16[512,1024]{1,0:T(8,128)(2,1)}) async-done(((bf16[128,3072]{1,0:T(8,128)(2,1)}, bf16[128,1024]{1,0:T(8,128)(2,1)}, bf16[128,4096]{1,0:T(8,128)(2,1)}, bf16[512,1024]{1,0:T(8,128)(2,1)}), (bf16[128,3072]{1,0:T(8,128)(2,1)}, bf16[128,1024]{1,0:T(8,128)(2,1)}, ...) | async-done | bytes 3145744 | tf_op jit(solution)/shard_map/psum | solution.py:468
  644.6 2.5 convert_element_type.27
  648.0 1.5 convert_element_type.29
  649.5 1.6 convert_element_type.30
  651.1 38.2 %all-reduce.5.cloned.1.call-done = (f32[8,1024]{1,0:T(8,128)}, f32[8,1024]{1,0:T(8,128)}) async-done(((f32[8,1024]{1,0:T(8,128)}, f32[8,1024]{1,0:T(8,128)}), (f32[8,1024]{1,0:T(8,128)}, f32[8,1024]{1,0:T(8,128)})) %all-reduce.5.cloned.1.call-update) | async-done | bytes 65552 | tf_op jit(solution)/shard_map/psum | solution.py:468
  (69 shorter events, 16.5 us)
Async XLA Ops:
  7.2 24.6 %copy-start = (f32[64,1024]{1,0:T(8,128)S(1)}, f32[64,1024]{1,0:T(8,128)}, u32[]{:S(2)}) copy-start(f32[64,1024]{1,0:T(8,128)} %param.20) | copy-start | bytes 786436
  7.2 238.8 %reduce-scatter.9.cloned.1.call-start = ((), (), s32[]{:S(2)}) async-start(), calls=%async_computation.7 | async-start | bytes 2359296 | tf_op jit(solution)/shard_map/reduce_scatter | solution.py:467
  7.3 7.2 %copy-start.4 = (bf16[4,256,1024]{2,1,0:T(8,128)(2,1)S(1)}, bf16[4,256,1024]{2,1,0:T(8,128)(2,1)}, u32[]{:S(2)}) copy-start(bf16[4,256,1024]{2,1,0:T(8,128)(2,1)} %param.13) | copy-start | bytes 6291460
  10.0 15.7 %collective-permute-start = (bf16[256,1024]{1,0:T(8,128)(2,1)S(1)}, bf16[256,1024]{1,0:T(8,128)(2,1)S(1)}, u32[]{:S(2)}, u32[]{:S(2)}) collective-permute-start(bf16[256,1024]{1,0:T(8,128)(2,1)S(1)} %get-tuple-element.68), channel_id=1, source_target_pairs={{0,8},{8,0},{16,24},{24,16},{1,9},{9,1},{17,25},{25,17},{2,10},{10... | collective-permute-start | bytes 1572872 | tf_op jit(solution)/shard_map/ppermute | solution.py:424
  12.9 26.2 %collective-permute-start.1 = (bf16[256,1024]{1,0:T(8,128)(2,1)S(1)}, bf16[256,1024]{1,0:T(8,128)(2,1)}, u32[]{:S(2)}, u32[]{:S(2)}) collective-permute-start(bf16[256,1024]{1,0:T(8,128)(2,1)S(1)} %get-tuple-element.70), channel_id=1, source_target_pairs={{0,16},{8,24},{16,0},{24,8},{1,17},{9,25},{17,1},{25,9},{2,18},{10... | collective-permute-start | bytes 1572872 | tf_op jit(solution)/shard_map/ppermute | solution.py:424
  14.4 14.3 %copy-start.11 = (s32[4]{0:T(128)S(1)}, s32[4]{0:T(128)}, u32[]{:S(2)}) copy-start(s32[4]{0:T(128)} %param.14) | copy-start | bytes 52
  14.4 24.7 %collective-permute-start.2 = (bf16[256,1024]{1,0:T(8,128)(2,1)S(1)}, bf16[256,1024]{1,0:T(8,128)(2,1)}, u32[]{:S(2)}, u32[]{:S(2)}) collective-permute-start(bf16[256,1024]{1,0:T(8,128)(2,1)S(1)} %get-tuple-element.67), channel_id=1, source_target_pairs={{0,24},{8,16},{16,8},{24,0},{1,25},{9,17},{17,9},{25,1},{2,26},{10... | collective-permute-start | bytes 1572872 | tf_op jit(solution)/shard_map/ppermute | solution.py:424
  15.5 68.5 %collective-permute-start.3 = (bf16[256,1024]{1,0:T(8,128)(2,1)S(1)}, bf16[256,1024]{1,0:T(8,128)(2,1)}, u32[]{:S(2)}, u32[]{:S(2)}) collective-permute-start(bf16[256,1024]{1,0:T(8,128)(2,1)S(1)} %get-tuple-element.64), channel_id=1, source_target_pairs={{0,8},{8,0},{16,24},{24,16},{1,9},{9,1},{17,25},{25,17},{2,10},{10... | collective-permute-start | bytes 1572872 | tf_op jit(solution)/shard_map/ppermute | solution.py:424
  17.5 66.6 %collective-permute-start.4 = (bf16[256,1024]{1,0:T(8,128)(2,1)S(1)}, bf16[256,1024]{1,0:T(8,128)(2,1)}, u32[]{:S(2)}, u32[]{:S(2)}) collective-permute-start(bf16[256,1024]{1,0:T(8,128)(2,1)S(1)} %get-tuple-element.66), channel_id=1, source_target_pairs={{0,16},{8,24},{16,0},{24,8},{1,17},{9,25},{17,1},{25,9},{2,18},{10... | collective-permute-start | bytes 1572872 | tf_op jit(solution)/shard_map/ppermute | solution.py:424
  25.7 13.4 %copy-start.7 = (bf16[256,1024]{1,0:T(8,128)(2,1)}, bf16[256,1024]{1,0:T(8,128)(2,1)S(1)}, u32[]{:S(2)}) copy-start(bf16[256,1024]{1,0:T(8,128)(2,1)S(1)} %collective-permute-done.refs_1_) | copy-start | bytes 1572868
  25.7 58.4 %collective-permute-start.5 = (bf16[256,1024]{1,0:T(8,128)(2,1)S(1)}, bf16[256,1024]{1,0:T(8,128)(2,1)}, u32[]{:S(2)}, u32[]{:S(2)}) collective-permute-start(bf16[256,1024]{1,0:T(8,128)(2,1)S(1)} %get-tuple-element.63), channel_id=1, source_target_pairs={{0,24},{8,16},{16,8},{24,0},{1,25},{9,17},{17,9},{25,1},{2,26},{10... | collective-permute-start | bytes 1572872 | tf_op jit(solution)/shard_map/ppermute | solution.py:424
  172.2 140.4 %reduce-scatter.7.cloned.1.call-start = ((), (), s32[]{:S(2)}) async-start(), calls=%async_computation.6 | async-start | bytes 7077888 | tf_op jit(solution)/shard_map/reduce_scatter | solution.py:467
  242.4 160.6 %reduce-scatter.11.cloned.1.call-start = ((), (), s32[]{:S(2)}) async-start(), calls=%async_computation.8 | async-start | bytes 9437184 | tf_op jit(solution)/shard_map/reduce_scatter | solution.py:467
  243.1 250.0 %reduce-scatter.13.cloned.1.call-start = ((), (), s32[]{:S(2)}) async-start(), calls=%async_computation.9 | async-start | bytes 9437184 | tf_op jit(solution)/shard_map/reduce_scatter | solution.py:467
  243.2 1.2 copy-start.9
  243.2 1.2 copy-start.10
  243.7 299.9 %reduce-scatter.15.cloned.1.call-start = ((), (), s32[]{:S(2)}) async-start(), calls=%async_computation.10 | async-start | bytes 294912 | tf_op jit(solution)/shard_map/reduce_scatter | solution.py:467
  244.4 249.0 %copy-start.3 = (bf16[1024,1024]{1,0:T(8,128)(2,1)S(1)}, bf16[1024,1024]{1,0:T(8,128)(2,1)}, u32[]{:S(2)}) copy-start(bf16[1024,1024]{1,0:T(8,128)(2,1)} %get-tuple-element.42) | copy-start | bytes 6291460
  245.3 309.9 %reduce-scatter.17.cloned.1.call-start = ((), (), s32[]{:S(2)}) async-start(), calls=%async_computation.11 | async-start | bytes 294912 | tf_op jit(solution)/shard_map/reduce_scatter | solution.py:467
  245.9 398.7 %all-reduce.7.cloned.1.call-start = ((), (), s32[]{:S(2)}) async-start(), calls=%async_computation.13 | async-start | bytes 6291456 | tf_op jit(solution)/shard_map/psum | solution.py:468
  493.1 196.2 %all-reduce.5.cloned.1.call-start = ((), (), s32[]{:S(2)}) async-start(), calls=%async_computation.12 | async-start | bytes 131072 | tf_op jit(solution)/shard_map/psum | solution.py:468
  493.4 3.8 copy-start.2
  493.6 15.8 %collective-permute-start.11 = (bf16[256,1024]{1,0:T(8,128)(2,1)S(1)}, bf16[256,1024]{1,0:T(8,128)(2,1)S(1)}, u32[]{:S(2)}, u32[]{:S(2)}) collective-permute-start(bf16[256,1024]{1,0:T(8,128)(2,1)S(1)} %get-tuple-element.56), channel_id=1, source_target_pairs={{0,24},{8,16},{16,8},{24,0},{1,25},{9,17},{17,9},{25,1},{2,26},{10... | collective-permute-start | bytes 1572872 | tf_op jit(solution)/shard_map/ppermute | solution.py:424
  496.0 24.7 %collective-permute-start.10 = (bf16[256,1024]{1,0:T(8,128)(2,1)S(1)}, bf16[256,1024]{1,0:T(8,128)(2,1)S(1)}, u32[]{:S(2)}, u32[]{:S(2)}) collective-permute-start(bf16[256,1024]{1,0:T(8,128)(2,1)S(1)} %get-tuple-element.57), channel_id=1, source_target_pairs={{0,16},{8,24},{16,0},{24,8},{1,17},{9,25},{17,1},{25,9},{2,18},{10... | collective-permute-start | bytes 1572872 | tf_op jit(solution)/shard_map/ppermute | solution.py:424
  496.6 24.1 %collective-permute-start.9 = (bf16[256,1024]{1,0:T(8,128)(2,1)S(1)}, bf16[256,1024]{1,0:T(8,128)(2,1)S(1)}, u32[]{:S(2)}, u32[]{:S(2)}) collective-permute-start(bf16[256,1024]{1,0:T(8,128)(2,1)S(1)} %get-tuple-element.58), channel_id=1, source_target_pairs={{0,8},{8,0},{16,24},{24,16},{1,9},{9,1},{17,25},{25,17},{2,10},{10... | collective-permute-start | bytes 1572872 | tf_op jit(solution)/shard_map/ppermute | solution.py:424
  498.3 33.8 %collective-permute-start.8 = (bf16[256,1024]{1,0:T(8,128)(2,1)}, bf16[256,1024]{1,0:T(8,128)(2,1)}, u32[]{:S(2)}, u32[]{:S(2)}) collective-permute-start(bf16[256,1024]{1,0:T(8,128)(2,1)} %get-tuple-element.60), channel_id=1, source_target_pairs={{0,24},{8,16},{16,8},{24,0},{1,25},{9,17},{17,9},{25,1},{2,26},{10... | collective-permute-start | bytes 1572872 | tf_op jit(solution)/shard_map/ppermute | solution.py:424
  500.7 39.2 %collective-permute-start.7 = (bf16[256,1024]{1,0:T(8,128)(2,1)}, bf16[256,1024]{1,0:T(8,128)(2,1)}, u32[]{:S(2)}, u32[]{:S(2)}) collective-permute-start(bf16[256,1024]{1,0:T(8,128)(2,1)} %get-tuple-element.61), channel_id=1, source_target_pairs={{0,16},{8,24},{16,0},{24,8},{1,17},{9,25},{17,1},{25,9},{2,18},{10... | collective-permute-start | bytes 1572872 | tf_op jit(solution)/shard_map/ppermute | solution.py:424
  509.4 30.5 %collective-permute-start.6 = (bf16[256,1024]{1,0:T(8,128)(2,1)S(1)}, bf16[256,1024]{1,0:T(8,128)(2,1)}, u32[]{:S(2)}, u32[]{:S(2)}) collective-permute-start(bf16[256,1024]{1,0:T(8,128)(2,1)S(1)} %get-tuple-element.62), channel_id=1, source_target_pairs={{0,8},{8,0},{16,24},{24,16},{1,9},{9,1},{17,25},{25,17},{2,10},{10... | collective-permute-start | bytes 1572872 | tf_op jit(solution)/shard_map/ppermute | solution.py:424
  644.6 2.5 copy-start.8
  644.6 3.4 copy-start.6
  647.1 2.4 copy-start.5
  648.0 44.1 %copy-start.1 = (f32[64,1024]{1,0:T(8,128)S(1)}, f32[64,1024]{1,0:T(8,128)}, u32[]{:S(2)}) copy-start(f32[64,1024]{1,0:T(8,128)} %param.20) | copy-start | bytes 786436
Sparse Core Ops, SparseCore 0:
  172.3 36.0 reduce-scatter.8
  242.5 70.1 reduce-scatter.6
  315.0 87.9 reduce-scatter.10
  405.1 87.9 reduce-scatter.12
  495.2 28.7 reduce-scatter.14
  526.7 28.4 reduce-scatter.16
  558.6 85.9 all-reduce.6
  647.7 41.5 all-reduce.4

commit v2 on v0

--- a/solution.py
+++ b/solution.py
@@ -1,38 +1,1316 @@
+import functools
 import math
 
 import jax
 import jax.numpy as jnp
 from jax import lax
+from jax.experimental import pallas as pl
+from jax.experimental.pallas import tpu as pltpu
 from jax.sharding import PartitionSpec as P
 
+F32 = jnp.float32
+BF16 = jnp.bfloat16
+HEAD = 64
 HEADS = 16
-
-
-def layer_norm(values_in):
+LOG2E = math.log2(math.e)
+GELU_C = math.sqrt(2 / math.pi)
+GELU_K = 0.044715
+VMEM = 63 * 2**20
+DOWN_SHARES = (0.65,)
+UP_SHARES = (0.5,)
+OUT_SHARES = (0.5,)
+QKV_SHARES = (0.5, 0.25)
+
+
+def dot(a, b, ca, cb):
+    return lax.dot_general(a, b, (((ca,), (cb,)), ((), ())), preferred_element_type=F32)
+
+
+def nn(a, b):
+    return dot(a, b, 1, 0)
+
+
+def nt(a, b):
+    return dot(a, b, 1, 1)
+
+
+def tn(a, b):
+    return dot(a, b, 0, 0)
+
+
+def whole(shape):
+    zeros = (0,) * len(shape)
+    return pl.BlockSpec(shape, lambda i: zeros, pipeline_mode=pl.Buffered(1))
+
+
+def params():
+    return pltpu.CompilerParams(vmem_limit_bytes=VMEM)
+
+
+def norm_rows(v):
+    centred = v - jnp.mean(v, axis=-1, keepdims=True)
+    inverse = lax.rsqrt(jnp.mean(centred * centred, axis=-1, keepdims=True) + 1e-05)
+    return centred * inverse, inverse
+
+
+def norm_back(g, normed, inverse):
+    first = jnp.mean(g, axis=-1, keepdims=True)
+    second = jnp.mean(g * normed, axis=-1, keepdims=True)
+    return inverse * (g - first - normed * second)
+
+
+def entry_kernel(ways, steps, *refs):
+    bins, live, tokens, gain_attn, gain_mlp, w, x_out, ready_out, packed_out, w_out, own_rows = refs[:11]
+    here, w_here, w_turned, ready_here, packed_here, send, recv, local, leave = refs[11:]
+    place = Place(ways, 0)
+    own_bin = bins[place.me]
+    gain = gain_attn[pl.ds(own_bin, 1)]
+    own_rows[0:1] = gain
+    own_rows[1:2] = gain_mlp[pl.ds(own_bin, 1)]
+    own_rows[2:3] = jnp.where(place.me < live[0], jnp.ones_like(gain), jnp.zeros_like(gain))
+    own_rows[3:8] = jnp.zeros((5, gain.shape[1]), F32)
+    rows, width = here.shape[1:]
+    cols = w_here.shape[1]
+    load_w = pltpu.make_async_copy(w, w_here, local.at[0])
+    load_own = pltpu.make_async_copy(tokens.at[place.me], here.at[0], local.at[1])
+    load_w.start()
+    load_own.start()
+
+    def move(k):
+        return pltpu.make_async_remote_copy(
+            src_ref=tokens.at[place.partner(k)], dst_ref=here.at[k],
+            send_sem=send.at[k], recv_sem=recv.at[k],
+            device_id=place.plane(k), device_id_type=MESH,
+        )
+
+    def span(k):
+        return pl.ds(k * rows, rows)
+
+    def leaving(k):
+        return [
+            pltpu.make_async_copy(here.at[k], x_out.at[span(k)], leave.at[0, k]),
+            pltpu.make_async_copy(ready_here.at[k], ready_out.at[:, span(k)], leave.at[1, k]),
+            pltpu.make_async_copy(packed_here.at[k], packed_out.at[:, span(k)], leave.at[2, k]),
+        ]
+
+    def project(k):
+        ready = (norm_rows(here[k].astype(F32))[0] * gain).astype(BF16)
+        ready_here[k] = ready.T
+        for c in range(0, cols, steps):
+            packed_here[k, c : c + steps] = nt(w_turned[c : c + steps], ready).astype(BF16)
+        for copy in leaving(k):
+            copy.start()
+
+    place.greet_plane()
+    for k in range(1, ways - 1):
+        move(k).start()
+    load_w.wait()
+
+    def turn(c, carry):
+        at = pl.ds(pl.multiple_of(c * 256, 256), 256)
+        w_turned[at] = w_here[:, at].T
+        return carry
+
+    lax.fori_loop(0, cols // 256, turn, 0)
+    save_w = pltpu.make_async_copy(w_turned, w_out, local.at[2])
+    save_w.start()
+    load_own.wait()
+    project(0)
+    for k in range(1, ways - 1):
+        move(k).wait_send()
+    move(ways - 1).start()
+    for k in range(1, ways):
+        move(k).wait_recv()
+        project(k)
+    move(ways - 1).wait_send()
+    save_w.wait()
+    for k in range(ways):
+        for copy in leaving(k):
+            copy.wait()
+
+
+def entry(bins, live, tokens, gain_attn, gain_mlp, w):
+    ways, rows, width = tokens.shape
+    cols = w.shape[1]
+    length = ways * rows
+    remote = pl.BlockSpec(memory_space=pl.ANY)
+    return pl.pallas_call(
+        functools.partial(entry_kernel, ways, math.gcd(cols, 1024)),
+        in_specs=[pl.BlockSpec(memory_space=pltpu.SMEM)] * 2
+        + [remote]
+        + [pl.BlockSpec(memory_space=pltpu.VMEM)] * 2
+        + [remote],
+        out_specs=[remote] * 4 + [pl.BlockSpec(memory_space=pltpu.VMEM)],
+        out_shape=[
+            jax.ShapeDtypeStruct((length, width), BF16),
+            jax.ShapeDtypeStruct((width, length), BF16),
+            jax.ShapeDtypeStruct((cols, length), BF16),
+            jax.ShapeDtypeStruct((cols, width), BF16),
+            jax.ShapeDtypeStruct((8, width), F32),
+        ],
+        scratch_shapes=[
+            pltpu.VMEM((ways, rows, width), BF16),
+            pltpu.VMEM((width, cols), BF16),
+            pltpu.VMEM((cols, width), BF16),
+            pltpu.VMEM((ways, width, rows), BF16),
+            pltpu.VMEM((ways, cols, rows), BF16),
+            pltpu.SemaphoreType.DMA((ways,)),
+            pltpu.SemaphoreType.DMA((ways,)),
+            pltpu.SemaphoreType.DMA((3,)),
+            pltpu.SemaphoreType.DMA((3, ways)),
+        ],
+        compiler_params=pltpu.CompilerParams(vmem_limit_bytes=VMEM, collective_id=0, has_side_effects=True),
+        name="entry",
+    )(bins, live, tokens, gain_attn, gain_mlp, w)
+
+
+def split2(v):
+    hi = v.astype(BF16)
+    return hi, (v - hi.astype(F32)).astype(BF16)
+
+
+def split3(v):
+    a = v.astype(BF16).astype(F32)
+    b = (v - a).astype(BF16).astype(F32)
+    return a, b, v - a - b
+
+
+def in_rows(rows, cols):
+    at = lax.broadcasted_iota(jnp.int32, (16, cols), 0)
+    out = jnp.zeros((16, cols), F32)
+    for i, row in enumerate(rows):
+        out = jnp.where(at == i, row, out)
+    return out.astype(BF16)
+
+
+def ones_rows(many, cols):
+    return (lax.broadcasted_iota(jnp.int32, (16, cols), 0) < many).astype(F32).astype(BF16)
+
+
+def head_parts(p, h):
+    base = 3 * HEAD * h
+    return [p[base + HEAD * j : base + HEAD * (j + 1)] for j in range(3)]
+
+
+def attend_kernel(p_ref, o_ref, aux_ref, *, bq):
+    length = p_ref.shape[1]
+
+    def run(exact):
+        work, low, high = [], [], []
+        for h in range(2):
+            q, k, v = head_parts(p_ref, h)
+            scaled = q.astype(F32) * (LOG2E * HEAD**-0.5)
+            qhi, qlo = split2(scaled)
+            if exact:
+                shift = None
+                qq = jnp.concatenate([qhi, qlo], axis=0)
+                kk = jnp.concatenate([k, k], axis=0).T
+            else:
+                k32 = k.astype(F32)
+                longest = jnp.sqrt(jnp.max(jnp.sum(k32 * k32, axis=0, keepdims=True)))
+                bound = jnp.sqrt(jnp.sum(scaled * scaled, axis=0, keepdims=True)) * longest
+                shift = bound.astype(BF16).astype(F32)
+                qq = jnp.concatenate([qhi, qlo, in_rows([-shift], length)], axis=0)
+                kk = jnp.concatenate([k, k, ones_rows(1, length)], axis=0).T
+            vv = jnp.concatenate([v, ones_rows(1, length)], axis=0)
+            for i in range(length // bq):
+                span = slice(i * bq, (i + 1) * bq)
+                work.append((h, span, kk, qq[:, span], vv, None if exact else shift[:, span]))
+        following = nn(work[0][2], work[0][3])
+        for n, (h, span, _, _, vv, m) in enumerate(work):
+            s = following
+            if n + 1 < len(work):
+                following = nn(work[n + 1][2], work[n + 1][3])
+            if exact:
+                m = jnp.max(s, axis=0, keepdims=True)
+                s = s - m
+            o = nn(vv, jnp.exp2(s).astype(BF16))
+            total = o[HEAD : HEAD + 1]
+            o_ref[HEAD * h : HEAD * (h + 1), span] = (o[:HEAD] * (1.0 / total)).astype(BF16)
+            aux_ref[h : h + 1, span] = -(m + jnp.log2(total))
+            low.append(jnp.min(total))
+            high.append(jnp.max(total))
+        return functools.reduce(jnp.minimum, low), functools.reduce(jnp.maximum, high)
+
+    low, high = run(False)
+    fine = (low > 2.0**-80) & (high < 2.0**80)
+
+    @pl.when(jnp.logical_not(fine))
+    def _():
+        run(True)
+
+
+def attend(packed):
+    cols, length = packed.shape
+    pairs = cols // (6 * HEAD)
+    return pl.pallas_call(
+        functools.partial(attend_kernel, bq=math.gcd(length, 256)),
+        grid=(pairs,),
+        in_specs=[pl.BlockSpec((6 * HEAD, length), lambda i: (i, 0))],
+        out_specs=[
+            pl.BlockSpec((2 * HEAD, length), lambda i: (i, 0)),
+            pl.BlockSpec((None, 8, length), lambda i: (i, 0, 0)),
+        ],
+        out_shape=[
+            jax.ShapeDtypeStruct((pairs * 2 * HEAD, length), BF16),
+            jax.ShapeDtypeStruct((pairs, 8, length), F32),
+        ],
+        compiler_params=params(),
+        name="attend",
+    )(packed)
+
+
+def attend_back_head(p_ref, o_ref, aux_ref, do_ref, bq, h):
+    length = p_ref.shape[1]
+    q, k, v = head_parts(p_ref, h)
+    do = do_ref[HEAD * h : HEAD * (h + 1)]
+    o = o_ref[HEAD * h : HEAD * (h + 1)]
+    qhi, qlo = split2(q.astype(F32) * (LOG2E * HEAD**-0.5))
+    qq = jnp.concatenate([qhi, qlo, in_rows(split3(aux_ref[h : h + 1]), length)], axis=0).T
+    kk = jnp.concatenate([k, k, ones_rows(3, length)], axis=0)
+    minus = -jnp.sum(do.astype(F32) * o.astype(F32), axis=0, keepdims=True)
+    dd = jnp.concatenate([do, in_rows(split3(minus), length)], axis=0).T
+    vv = jnp.concatenate([v, ones_rows(3, length)], axis=0)
+    dv = jnp.zeros((HEAD, length), F32)
+    dk = jnp.zeros((HEAD, length), F32)
+    dq = []
+    spans = [slice(i * bq, (i + 1) * bq) for i in range(length // bq)]
+    following = nn(qq[spans[0]], kk), nn(dd[spans[0]], vv)
+    for i, span in enumerate(spans):
+        s, g = following
+        if i + 1 < len(spans):
+            following = nn(qq[spans[i + 1]], kk), nn(dd[spans[i + 1]], vv)
+        p = jnp.exp2(s)
+        ds = (p * g).astype(BF16)
+        dv = dv + nn(do[:, span], p.astype(BF16))
+        dk = dk + nn(q[:, span], ds)
+        dq.append((nt(k, ds) * HEAD**-0.5).astype(BF16))
+    return [jnp.concatenate(dq, axis=1), (dk * HEAD**-0.5).astype(BF16), dv.astype(BF16)]
+
+
+MESH = pl.DeviceIdType.MESH
+
+
+class Place:
+    def __init__(self, ways, line):
+        self.ways, self.line = ways, line
+        self.me = lax.axis_index("seq")
+        self.b = lax.axis_index("batch")
+        self.core = lax.rem(self.b, 2)
+        self.z = self.b // 2
+
+    def other_core(self):
+        return {"batch": self.b + 1 - 2 * self.core}
+
+    def along(self, step):
+        return {"batch": self.b + 2 * step}
+
+    def plane(self, k):
+        return {"seq": self.partner(k)}
+
+    def partner(self, k):
+        out = self.me
+        for bit in range(k.bit_length()):
+            if k >> bit & 1:
+                out = out + (1 << bit) * (1 - 2 * lax.rem(self.me // (1 << bit), 2))
+        return out
+
+    def greet_core(self):
+        barrier = pltpu.get_barrier_semaphore()
+        pl.semaphore_signal(barrier, inc=1, device_id=self.other_core(), device_id_type=MESH)
+        pl.semaphore_wait(barrier, 1)
+
+    def greet_plane(self):
+        barrier = pltpu.get_barrier_semaphore()
+        for k in range(1, self.ways):
+            pl.semaphore_signal(barrier, inc=1, device_id=self.plane(k), device_id_type=MESH)
+        pl.semaphore_wait(barrier, self.ways - 1)
+
+    def hail(self):
+        barrier = pltpu.get_barrier_semaphore()
+
+        def tell(where):
+            pl.semaphore_signal(barrier, inc=1, device_id=where, device_id_type=MESH)
+
+        tell(self.other_core())
+        for k in range(1, self.ways):
+            tell(self.plane(k))
+
+        @pl.when(self.z > 0)
+        def _():
+            tell(self.along(-1))
+
+        @pl.when(self.z < self.line - 1)
+        def _():
+            tell(self.along(1))
+
+    def greet(self):
+        ends = (self.z == 0).astype(jnp.int32) + (self.z == self.line - 1).astype(jnp.int32)
+        pl.semaphore_wait(pltpu.get_barrier_semaphore(), self.ways + 2 - ends)
+
+
+def add_rows(dst, srcs, rows, cols):
+    step = row_step(rows, cols)
+
+    def one(i, carry):
+        at = pl.multiple_of(i * step, step)
+        total = dst(at, step)[...]
+        for src in srcs:
+            total = total + src(at, step)[...]
+        dst(at, step)[...] = total
+        return carry
+
+    lax.fori_loop(0, rows // step, one, 0)
+
+
+def row_step(rows, cols):
+    for step in (64, 48, 32):
+        if rows % step == 0 and step * cols <= 32768:
+            return step
+    return 16
+
+
+class Way:
+    def __init__(self, place, order, part):
+        bits = lax.rem(place.me, 2), place.me // 2
+        self.a, self.b = (bits[0], bits[1]) if order == 0 else (bits[1], bits[0])
+        self.first, self.second = (1, 2) if order == 0 else (2, 1)
+        self.part = part
+
+    def half(self, a):
+        return pl.ds(pl.multiple_of(a * 2 * self.part, 2 * self.part), 2 * self.part)
+
+    def quarter(self, a, b):
+        return pl.ds(pl.multiple_of((2 * a + b) * self.part, self.part), self.part)
+
+
+class Reduce:
+    def __init__(self, ways, line, rows, cols, split, first, paired, does):
+        self.ways, self.line, self.rows, self.cols, self.split = ways, line, rows, cols, split
+        self.front, self.back = does != "back", does != "front"
+        self.here = pl.ds(first, cols)
+        self.part = cols // 4
+        self.paired = paired
+
+    def buffers(self):
+        line, rows, cols, split, part = self.line, self.rows, self.cols, self.split, self.part
+        hops, rest = line - 1, rows - split
+        shapes = {}
+        if self.front:
+            shapes["own"] = (line, rows, cols)
+            if not self.paired:
+                shapes["near"] = (line, rows, cols)
+            if rest:
+                shapes["z_right"] = shapes["z_left"] = (hops, rest, cols)
+            if split:
+                shapes["x_half"] = (line, split, 2 * part)
+        if self.back:
+            if rest:
+                shapes["z_half"] = (rest, 2 * part)
+                shapes["z_part"] = (rest, part)
+                if not self.front:
+                    shapes["z_row"] = (rest, cols)
+            if split:
+                shapes["x_right"] = shapes["x_left"] = (hops, split, part)
+            shapes["final"] = (rows, cols)
+        if split:
+            shapes["x_part"] = (line, split, part)
+        return shapes
+
+    def scratch(self):
+        n = 2 + 2 * 2 * (self.line - 1) + 2 * 8
+        return [pltpu.VMEM(shape, BF16) for shape in self.buffers().values()] + [
+            pltpu.SemaphoreType.DMA((n,)),
+            pltpu.SemaphoreType.DMA((n,)),
+        ]
+
+    def bind(self, place, source, final, refs):
+        refs = list(refs)
+        self.place, self.source, self.result = place, source, final
+        for name in self.buffers():
+            setattr(self, name, refs.pop(0))
+        self.send, self.recv = refs
+        self.orders = [Way(place, order, self.part) for order in (0, 1)]
+        self.ids = {}
+        return self
+
+    def copy(self, key, src, dst, where):
+        n = self.ids.setdefault(key, len(self.ids) + 1)
+        return pltpu.make_async_remote_copy(
+            src_ref=src, dst_ref=dst, send_sem=self.send.at[n], recv_sem=self.recv.at[n],
+            device_id=where, device_id_type=MESH,
+        )
+
+    def core_copy(self):
+        p = self.place
+        return self.copy("core", self.source.at[:, 1 - p.core, :, self.here], self.near, p.other_core())
+
+    def own_copy(self):
+        p = self.place
+        if self.paired:
+            return pltpu.make_async_copy(self.source.at[:, :, self.here], self.own, self.send.at[0])
+        return pltpu.make_async_copy(self.source.at[:, p.core, :, self.here], self.own, self.send.at[0])
+
+    def done_copy(self):
+        return pltpu.make_async_copy(self.final, self.result.at[:, self.here], self.send.at[0])
+
+    def kind_rows(self, kind):
+        return (0, self.split) if kind == "x" else (self.split, self.rows - self.split)
+
+    def mine(self, kind, start, many, columns):
+        if kind == "x":
+            return self.own.at[:, pl.ds(start, many), columns]
+        if not self.front:
+            return self.z_row.at[pl.ds(start - self.split, many), columns]
+        return self.own.at[self.place.z, pl.ds(start, many), columns]
+
+    def landing(self, buffer, kind, start, many):
+        return buffer.at[:, pl.ds(start, many)] if kind == "x" else buffer.at[pl.ds(start, many)]
+
+    def scatter(self, kind, stage, order):
+        way = self.orders[order]
+        first, many = self.kind_rows(kind)
+        many = many // 2
+        at = order * many
+        if stage == 1:
+            columns, where, buffer = way.half(1 - way.a), way.first, self.x_half if kind == "x" else self.z_half
+        else:
+            columns, where, buffer = way.quarter(way.a, 1 - way.b), way.second, self.x_part if kind == "x" else self.z_part
+        return self.copy(
+            (kind, "scatter", stage, order),
+            self.mine(kind, first + at, many, columns),
+            self.landing(buffer, kind, at, many),
+            self.place.plane(where),
+        )
+
+    def gather(self, kind, stage, order, arriving=False):
+        way = self.orders[order]
+        first, many = self.kind_rows(kind)
+        many = many // 2
+        rows = pl.ds(first + order * many, many)
+        if stage == 1:
+            columns, where = way.quarter(way.a, 1 - way.b if arriving else way.b), way.second
+        else:
+            columns, where = way.half(1 - way.a if arriving else way.a), way.first
+        view = self.final.at[rows, columns]
+        return self.copy((kind, "gather", stage, order), view, view, self.place.plane(where))
+
+    def scatter_start(self, kind, stage):
+        for order in (0, 1):
+            self.scatter(kind, stage, order).start()
+
+    def scatter_add(self, kind, stage):
+        first, many = self.kind_rows(kind)
+        many = many // 2
+        for order in (0, 1):
+            self.scatter(kind, stage, order).wait_recv()
+        for order in (0, 1):
+            way = self.orders[order]
+            at = order * many
+            columns = way.half(way.a) if stage == 1 else way.quarter(way.a, way.b)
+            if kind == "x":
+                buffer = self.x_half if stage == 1 else self.x_part
+
+                def each(j, carry, buffer=buffer, columns=columns, at=at):
+                    here = lambda r, n: self.own.at[j, pl.ds(first + at + r, n), columns]
+                    came = lambda r, n: buffer.at[j, pl.ds(at + r, n)]
+                    add_rows(*((here, [came]) if stage == 1 else (came, [here])), many, buffer.shape[-1])
+                    return carry
+
+                lax.fori_loop(0, self.line, each, 0)
+            else:
+                buffer = self.z_half if stage == 1 else self.z_part
+                here = lambda r, n, at=at, columns=columns: self.mine("z", first + at + r, n, columns)
+                came = lambda r, n, at=at, buffer=buffer: buffer.at[pl.ds(at + r, n)]
+                add_rows(*((here, [came]) if stage == 1 else (came, [here])), many, buffer.shape[-1])
+
+    def gather_start(self, kind, stage):
+        if stage == 1:
+            first, many = self.kind_rows(kind)
+            many = many // 2
+            for order in (0, 1):
+                way = self.orders[order]
+                rows = pl.ds(order * many, many)
+                done = self.x_part[self.place.z, rows] if kind == "x" else self.z_part[rows]
+                self.final[pl.ds(first + order * many, many), way.quarter(way.a, way.b)] = done
+        for order in (0, 1):
+            if stage == 2:
+                self.gather(kind, 1, order, True).wait_recv()
+            self.gather(kind, stage, order).start()
+
+    def line_row(self, kind, j):
+        if kind == "x":
+            return self.x_part.at[j]
+        return self.own.at[j, pl.ds(self.split, self.rows - self.split)]
+
+    def line_in(self, kind, right):
+        if kind == "x":
+            return self.x_right if right else self.x_left
+        return self.z_right if right else self.z_left
+
+    def line_copy(self, kind, right, t, j):
+        return self.copy(
+            (kind, right, t),
+            self.line_row(kind, j),
+            self.line_in(kind, right).at[t - 1],
+            self.place.along(1 if right else -1),
+        )
+
+    def line_step(self, kind, t):
+        p, line = self.place, self.line
+        for right in (True, False):
+            at = p.z if right else line - 1 - p.z
+            if t < line:
+                j = line + p.z - t if right else p.z + t - line
+
+                @pl.when(at <= t - 1)
+                def _(right=right, at=at, j=j):
+                    if t > 1:
+
+                        @pl.when(at >= 1)
+                        def _():
+                            self.line_arrive(kind, right, t - 1, j)
+
+                    self.line_copy(kind, right, t, j).start()
+
+            else:
+
+                @pl.when(at >= 1)
+                def _(right=right):
+                    self.line_arrive(kind, right, t - 1, p.z)
+
+    def line_arrive(self, kind, right, t, j):
+        buffer = self.line_in(kind, right)
+        self.copy(
+            (kind, right, t),
+            self.line_row(kind, j),
+            buffer.at[t - 1],
+            self.place.along(-1 if right else 1),
+        ).wait_recv()
+        if kind == "x":
+            mine = lambda r, n: self.x_part.at[j, pl.ds(r, n)]
+        else:
+            mine = lambda r, n: self.own.at[j, pl.ds(self.split + r, n)]
+        add_rows(mine, [lambda r, n: buffer.at[t - 1, pl.ds(r, n)]], self.kind_rows(kind)[1], buffer.shape[-1])
+
+    def line_sent(self, kind):
+        p, line = self.place, self.line
+        for t in range(1, line):
+            for right in (True, False):
+                at = p.z if right else line - 1 - p.z
+
+                @pl.when(at <= t - 1)
+                def _(right=right, t=t):
+                    self.line_copy(kind, right, t, p.z).wait_send()
+
+    def saved(self):
+        shapes = []
+        if self.rows - self.split:
+            shapes.append((self.rows - self.split, self.cols))
+        if self.split:
+            shapes.append((self.line, self.split, self.part))
+        return shapes
+
+    def save(self, refs):
+        refs = list(refs)
+        if self.rows - self.split:
+            refs.pop(0)[...] = self.own[self.place.z, pl.ds(self.split, self.rows - self.split)]
+        if self.split:
+            refs.pop(0)[...] = self.x_part[...]
+
+    def resume(self, refs):
+        refs = list(refs)
+        if self.rows - self.split:
+            self.z_row[...] = refs.pop(0)[...]
+        if self.split:
+            self.x_part[...] = refs.pop(0)[...]
+
+    def phase(self, n):
+        x, z = bool(self.split), bool(self.rows - self.split)
+        if n == 0:
+            self.own_copy().start()
+            if not self.paired:
+                self.core_copy().start()
+        if n == 1:
+            self.own_copy().wait()
+            if not self.paired:
+                self.core_copy().wait_recv()
+
+                def one(j, carry):
+                    add_rows(
+                        lambda r, n: self.own.at[j, pl.ds(r, n)],
+                        [lambda r, n: self.near.at[j, pl.ds(r, n)]],
+                        self.rows,
+                        self.cols,
+                    )
+                    return carry
+
+                lax.fori_loop(0, self.line, one, 0)
+            if x:
+                self.scatter_start("x", 1)
+        if z and 1 <= n <= 4:
+            self.line_step("z", n)
+        if x and n == 3:
+            self.scatter_add("x", 1)
+            self.scatter_start("x", 2)
+        if n == 4:
+            if x:
+                self.scatter_add("x", 2)
+                for order in (0, 1):
+                    for stage in (1, 2):
+                        self.scatter("x", stage, order).wait_send()
+            if z:
+                self.line_sent("z")
+            if not self.paired:
+                self.core_copy().wait_send()
+        if z and n == 5:
+            self.scatter_start("z", 1)
+        if x and 5 <= n <= 8:
+            self.line_step("x", n - 4)
+        if z and n == 6:
+            self.scatter_add("z", 1)
+            self.scatter_start("z", 2)
+        if z and n == 7:
+            self.scatter_add("z", 2)
+            self.gather_start("z", 1)
+        if n == 8:
+            if x:
+                self.gather_start("x", 1)
+            if z:
+                self.gather_start("z", 2)
+        if x and n == 9:
+            self.gather_start("x", 2)
+        if n == 10:
+            for kind, there in (("x", x), ("z", z)):
+                if there:
+                    for order in (0, 1):
+                        self.gather(kind, 2, order, True).wait_recv()
+                        for stage in (1, 2):
+                            self.gather(kind, stage, order).wait_send()
+                            if kind == "z":
+                                self.scatter(kind, stage, order).wait_send()
+            if x:
+                self.line_sent("x")
+            self.done_copy().start()
+        if n == 11:
+            self.done_copy().wait()
+
+
+class Sums:
+    def __init__(self, ways, line, rows, cols, shares, plan, paired=False, does="all"):
+        width = cols // len(shares)
+        self.shape, self.plan, self.does = (rows, cols), plan, does
+        self.parts = [
+            Reduce(ways, line, rows, width, int(rows * share) // 32 * 32, i * width, paired, does)
+            for i, share in enumerate(shares)
+        ]
+
+    def out(self):
+        if self.does == "front":
+            return [(whole(v), jax.ShapeDtypeStruct(v, BF16)) for part in self.parts for v in part.saved()]
+        return [(pl.BlockSpec(memory_space=pl.ANY), jax.ShapeDtypeStruct(self.shape, BF16))]
+
+    def ins(self):
+        if self.does == "back":
+            return [whole(v) for part in self.parts for v in part.saved()]
+        return [pl.BlockSpec(memory_space=pl.ANY)]
+
+    def scratch(self):
+        return [s for part in self.parts for s in part.scratch()]
+
+    def bind(self, place, sources, finals, refs):
+        refs = list(refs)
+        self.sources, self.finals = sources, finals
+        for part in self.parts:
+            many = len(part.scratch())
+            part.bind(place, sources[0], finals[0], refs[:many])
+            refs = refs[many:]
+
+    def phase(self, n):
+        if n == 5 and self.does == "back":
+            refs = list(self.sources)
+            for part in self.parts:
+                many = len(part.saved())
+                part.resume(refs[:many])
+                refs = refs[many:]
+        for part in self.parts:
+            part.phase(n)
+        if n == 4 and self.does == "front":
+            refs = list(self.finals)
+            for part in self.parts:
+                many = len(part.saved())
+                part.save(refs[:many])
+                refs = refs[many:]
+
+
+class Swap:
+    def __init__(self, ways, rows, cols, plan):
+        self.ways, self.shape, self.plan = ways, (ways, rows, cols), plan
+
+    def scratch(self):
+        return [pltpu.SemaphoreType.DMA((self.ways,)), pltpu.SemaphoreType.DMA((self.ways,))]
+
+    def out(self):
+        return [(pl.BlockSpec(memory_space=pl.ANY), jax.ShapeDtypeStruct(self.shape, BF16))]
+
+    def ins(self):
+        return [pl.BlockSpec(memory_space=pl.ANY)]
+
+    def bind(self, place, sources, finals, refs):
+        self.place, self.source, self.final = place, sources[0], finals[0]
+        self.send, self.recv = refs
+
+    def copy(self, k, slot):
+        return pltpu.make_async_remote_copy(
+            src_ref=self.source.at[k], dst_ref=self.final.at[slot],
+            send_sem=self.send.at[k], recv_sem=self.recv.at[k],
+            device_id=self.place.plane(k), device_id_type=MESH,
+        )
+
+    def stay(self):
+        return pltpu.make_async_copy(self.source.at[0], self.final.at[self.place.me], self.send.at[0])
+
+    def phase(self, n):
+        p = self.place
+        if n == 0:
+            self.stay().start()
+            for k in range(1, self.ways - 1):
+                self.copy(k, p.me).start()
+        if n == 1:
+            self.copy(self.ways - 1, p.me).start()
+        if n == 2:
+            self.stay().wait()
+            for k in range(1, self.ways):
+                self.copy(k, p.partner(k)).wait_recv()
+                self.copy(k, p.me).wait_send()
+
+
+class PairSum:
+    def __init__(self, line, rows, cols, steps, piece, cut):
+        self.shape, self.steps, self.piece, self.cut = (line, rows, cols), steps, piece, cut
+
+    def out(self):
+        return pl.BlockSpec(memory_space=pl.ANY), jax.ShapeDtypeStruct(self.shape, BF16)
+
+    def scratch(self):
+        line, rows, cols = self.piece
+        sems = [pltpu.SemaphoreType.DMA((self.steps,))] * 3
+        return [pltpu.VMEM((3, line, 2, rows, cols), BF16), pltpu.VMEM(self.shape, BF16)] + sems
+
+    def bind(self, place, final, refs):
+        self.place, self.final = place, final
+        self.stage, self.near, self.send, self.recv, self.leave = refs
+
+    def copy(self, i):
+        p = self.place
+        return pltpu.make_async_remote_copy(
+            src_ref=self.stage.at[lax.rem(i, 3), :, 1 - p.core], dst_ref=self.near.at[self.cut(i)],
+            send_sem=self.send.at[i], recv_sem=self.recv.at[i],
+            device_id=p.other_core(), device_id_type=MESH,
+        )
+
+    def leaving(self, i):
+        at = self.cut(i)
+        return pltpu.make_async_copy(self.near.at[at], self.final.at[at], self.leave.at[i])
+
+    def push(self, i, value):
+        line, rows, cols = self.piece
+        self.stage[lax.rem(i, 3)] = value.reshape(line, 2, rows, cols)
+        self.copy(i).start()
+
+    def take_late(self, i):
+        pl.when(i >= 2)(lambda: self.take(i - 2))
+
+    def take_rest(self, i):
+        self.take(i - 1)
+        self.take(i)
+        for n in range(self.steps):
+            self.leaving(n).wait()
+
+    def take(self, i):
+        line, rows, cols = self.piece
+        self.copy(i).wait_recv()
+        self.copy(i).wait_send()
+        at = self.cut(i)
+        for j in range(line):
+            here = (pl.ds(at[0].start + j, 1),) + at[1:]
+            self.near[here] = (self.stage[lax.rem(i, 3), j, self.place.core] + self.near[here][0])[None]
+        self.leaving(i).start()
+
+
+class Side:
+    def __init__(self, ways, line, jobs):
+        self.ways, self.line, self.jobs = ways, line, jobs
+
+    def in_specs(self):
+        return [spec for job in self.jobs for spec in job.ins()]
+
+    def out_specs(self):
+        return [spec for job in self.jobs for spec, _ in job.out()]
+
+    def out_shape(self):
+        return [shape for job in self.jobs for _, shape in job.out()]
+
+    def scratch(self):
+        return [s for job in self.jobs for s in job.scratch()]
+
+    def bind(self, sources, finals, refs):
+        refs, finals = list(refs), list(finals)
+        self.place = Place(self.ways, self.line)
+        for job, source in zip(self.jobs, sources):
+            many, outs = len(job.scratch()), len(job.out())
+            job.bind(self.place, source, finals[:outs], refs[:many])
+            refs, finals = refs[many:], finals[outs:]
+
+    def at(self, i, point):
+        for job in self.jobs:
+            for n in range(12):
+                if n in job.plan and job.plan[n][1] == point:
+                    if isinstance(i, int):
+                        job.phase(n)
+                    else:
+                        pl.when(i == job.plan[n][0])(functools.partial(job.phase, n))
+
+
+def remote_params(ident):
+    return pltpu.CompilerParams(vmem_limit_bytes=VMEM, collective_id=ident, has_side_effects=True)
+
+
+def mlp_kernel(pieces, *refs):
+    x, mixed, w_out, own_rows = refs[:4]
+    cots = refs[4 : 4 + pieces]
+    w_up, hidden, ready, gout, act, slope, grad_down = refs[4 + pieces :]
+    rows = cots[0].shape[0]
+
+    @pl.when(pl.program_id(0) == 0)
+    def _():
+        for k in range(pieces):
+            span = slice(k * rows, (k + 1) * rows)
+            gout[span] = cots[k][...] * own_rows[2:3].astype(BF16)
+            h = x[span].astype(F32) + tn(mixed[:, span], w_out[...])
+            hidden[span] = h
+            ready[span] = (norm_rows(h)[0] * own_rows[1:2]).astype(BF16)
+
+    u = nn(ready[...], w_up[...])
+    u2 = u * u
+    t = jnp.tanh(u * (GELU_C + (GELU_C * GELU_K) * u2))
+    half = 0.5 + 0.5 * t
+    a = (u * half).astype(BF16)
+    act[...] = a
+    slope[...] = (half + u * (1 - t * t) * (0.5 * GELU_C + (1.5 * GELU_C * GELU_K) * u2)).astype(BF16)
+    grad_down[...] = tn(a, gout[...]).astype(BF16)
+
+
+def mlp(x, mixed, w_out, own_rows, cots, w_up):
+    length, width = x.shape
+    inner = w_up.shape[1]
+    rows = length // len(cots)
+    block = min(1024, inner)
+    cols = pl.BlockSpec((length, block), lambda i: (0, i))
+    return pl.pallas_call(
+        functools.partial(mlp_kernel, len(cots)),
+        grid=(inner // block,),
+        in_specs=[
+            whole((length, width)),
+            whole((length, width)),
+            whole((width, width)),
+            whole((8, width)),
+        ]
+        + [whole((rows, width))] * len(cots)
+        + [pl.BlockSpec((width, block), lambda i: (0, i))],
+        out_specs=[whole((length, width))] * 3 + [cols, cols, pl.BlockSpec((block, width), lambda i: (i, 0))],
+        out_shape=[
+            jax.ShapeDtypeStruct((length, width), F32),
+            jax.ShapeDtypeStruct((length, width), BF16),
+            jax.ShapeDtypeStruct((length, width), BF16),
+            jax.ShapeDtypeStruct((length, inner), BF16),
+            jax.ShapeDtypeStruct((length, inner), BF16),
+            jax.ShapeDtypeStruct((inner, width), BF16),
+        ],
+        compiler_params=params(),
+        name="mlp",
+    )(x, mixed, w_out, own_rows, *cots, w_up)
+
+
+def mlp_back_kernel(side, *refs):
+    gout, act, slope, w_down, ready, hidden, source = refs[:7]
+    many = len(side.out_shape())
+    out, grad_upward, grad_up = refs[7:10]
+    out_sum = refs[10 + many]
+    side.bind([[source]], refs[10 : 10 + many], refs[11 + many :])
+    i = pl.program_id(0)
+    last = pl.num_programs(0) - 1
+
+    @pl.when(i == 0)
+    def _():
+        side.place.hail()
+        out_sum[...] = hidden[...]
+        side.place.greet()
+
+    side.at(i, 0)
+    gu = (nt(gout[...], w_down[...]) * slope[...].astype(F32)).astype(BF16)
+    grad_upward[...] = gu
+    grad_up[...] = tn(ready[...], gu).astype(BF16)
+    side.at(i, 1)
+    out_sum[...] += nn(act[...], w_down[...])
+
+    @pl.when(i == last)
+    def _():
+        out[...] = out_sum[...].astype(BF16)
+        side.at(i, "end")
+
+
+def mlp_back(gout, act, slope, w_down, ready, hidden, grad_down, ways):
+    length, width = gout.shape
+    inner = w_down.shape[0]
+    line, _, down_rows, _ = grad_down.shape
+    block = inner // 8
+    cols = pl.BlockSpec((length, block), lambda i: (0, i))
+    square = whole((length, width))
+    plan = {0: (0, 0), 1: (2, 0), 2: (4, 1), 3: (7, 0), 4: (7, "end")}
+    side = Side(ways, line, [Sums(ways, line, down_rows, width, DOWN_SHARES, plan, False, "front")])
+    return pl.pallas_call(
+        functools.partial(mlp_back_kernel, side),
+        grid=(8,),
+        in_specs=[
+            square,
+            cols,
+            cols,
+            pl.BlockSpec((block, width), lambda i: (i, 0)),
+            square,
+            square,
+        ]
+        + side.in_specs(),
+        out_specs=[square, cols, pl.BlockSpec((width, block), lambda i: (0, i))] + side.out_specs(),
+        out_shape=[
+            jax.ShapeDtypeStruct((length, width), BF16),
+            jax.ShapeDtypeStruct((length, inner), BF16),
+            jax.ShapeDtypeStruct((width, inner), BF16),
+        ]
+        + side.out_shape(),
+        scratch_shapes=[pltpu.VMEM((length, width), F32)] + side.scratch(),
+        compiler_params=remote_params(2),
+        name="mlp_back",
+    )(gout, act, slope, w_down, ready, hidden, grad_down)
+
+
+def attn_back_kernel(side, pair_sum, bq, *refs):
+    gu, w_up, hidden, gout, own_rows, mixed, w_out, packed, aux, w_qkv, ready, x = refs[:12]
+    back_from = len(side.jobs[0].ins())
+    carried, source_up, source_out = refs[12 : 12 + back_from], refs[12 + back_from], refs[13 + back_from]
+    refs = refs[14 + back_from :]
+    grad_qkv, grad_x, table_attn, table_mlp = refs[:4]
+    many = len(side.out_shape())
+    finals, refs = refs[4 : 4 + many], refs[4 + many :]
+    back_sum, grad_hidden, grad_mixed, spare, grad_out, late = refs[:6]
+    pairing = len(pair_sum.scratch())
+    side.bind([carried, [source_up], [grad_out], [source_out]], finals, refs[6 + pairing :])
+    pair_sum.bind(side.place, grad_qkv, refs[6 : 6 + pairing])
+    i = pl.program_id(0)
+    steps = pl.num_programs(0) // 2
+    length, width = gout.shape
+    span = math.gcd(length, 256)
+    load_hidden = pltpu.make_async_copy(hidden, grad_hidden, late.at[0])
+    load_w = pltpu.make_async_copy(w_out, spare, late.at[1])
+    load_gout = pltpu.make_async_copy(gout, grad_x, late.at[2])
+    load_x = pltpu.make_async_copy(x, spare, late.at[3])
+
+    @pl.when(i == 0)
+    def _():
+        side.place.hail()
+        load_hidden.start()
+        load_w.start()
+        load_gout.start()
+        back_sum[...] = jnp.zeros_like(back_sum)
+
+    pl.when(i == 1)(side.place.greet)
+    side.at(i, 0)
+
+    @pl.when(i < steps)
+    def _():
+        back_sum[...] += nt(gu[...], w_up[...])
+
+    @pl.when(i == steps - 1)
+    def _():
+        load_hidden.wait()
+        load_w.wait()
+        load_gout.wait()
+        total = jnp.zeros((1, width), F32)
+        for r in range(length // span):
+            here = slice(r * span, (r + 1) * span)
+            normed, inverse = norm_rows(grad_hidden[here])
+            g = back_sum[here]
+            total = total + jnp.sum(g * normed, axis=0, keepdims=True)
+            grad_hidden[here] = grad_x[here].astype(F32) + norm_back(g * own_rows[1:2], normed, inverse)
+        table_mlp[...] = total
+        side.at(i, "norm")
+        low = grad_hidden[...].astype(BF16)
+        grad_mixed[...] = nt(spare[...], low).astype(BF16)
+        load_x.start()
+        grad_out[...] = nn(mixed[...], low).astype(BF16).reshape(grad_out.shape)
+        back_sum[...] = jnp.zeros_like(back_sum)
+        side.at(i, "out")
+
+    @pl.when(i >= steps)
+    def _():
+        pair = i - steps
+        pair_sum.take_late(pair)
+        rows = pl.ds(pl.multiple_of(pair * 2 * HEAD, 2 * HEAD), 2 * HEAD)
+        parts = attend_back_head(packed, mixed[rows], aux, grad_mixed[rows], bq, 0)
+        side.at(i, "mid")
+        parts = parts + attend_back_head(packed, mixed[rows], aux, grad_mixed[rows], bq, 1)
+        side.at(i, 1)
+        gp = jnp.concatenate(parts, axis=0)
+        pair_sum.push(pair, nt(ready[...], gp).astype(BF16))
+        back_sum[...] += tn(gp, w_qkv[...])
+        side.at(i, 2)
+
+    @pl.when(i == pl.num_programs(0) - 1)
+    def _():
+        load_x.wait()
+        total = jnp.zeros((1, width), F32)
+        for r in range(length // span):
+            here = slice(r * span, (r + 1) * span)
+            normed, inverse = norm_rows(spare[here].astype(F32))
+            g = back_sum[here]
+            total = total + jnp.sum(g * normed, axis=0, keepdims=True)
+            grad_x[here] = (grad_hidden[here] + norm_back(g * own_rows[0:1], normed, inverse)).astype(BF16)
+        table_attn[...] = total
+        pair_sum.take_rest(i - steps)
+        side.at(i, "end")
+
+
+def attn_back(gu, w_up, hidden, gout, own_rows, mixed, w_out, packed, aux, w_qkv, ready, x, carried, grad_up, out, ways):
+    length, width = gout.shape
+    inner = w_up.shape[1]
+    cols = packed.shape[0]
+    pairs = cols // (6 * HEAD)
+    line, _, rows, _ = grad_up.shape
+    block = inner // pairs
+    square = whole((length, width))
+    remote = pl.BlockSpec(memory_space=pl.ANY)
+    first = lambda i: jnp.minimum(i, pairs - 1)
+    second = lambda i: jnp.maximum(i - pairs, 0)
+    plan_down = {5: (1, 0), 6: (5, 0), 7: (7, 0), 8: (7, "norm"), 9: (8, "mid"), 10: (9, 0), 11: (15, "end")}
+    plan_up = {
+        0: (1, 0), 1: (7, 0), 2: (8, 1), 3: (10, "mid"), 4: (12, 1), 5: (12, 1),
+        6: (13, 0), 7: (13, 1), 8: (14, 0), 9: (14, "mid"), 10: (15, 0), 11: (15, "end"),
+    }
+    plan_out = {
+        0: (7, "out"), 1: (8, "mid"), 2: (9, "mid"), 3: (11, 0), 4: (12, 2), 5: (12, 2),
+        6: (13, "mid"), 7: (13, 2), 8: (14, "mid"), 9: (14, 1), 10: (15, "mid"), 11: (15, "end"),
+    }
+    plan_swap = {0: (8, "mid"), 1: (10, 1), 2: (15, 1)}
+    side = Side(
+        ways,
+        line,
+        [
+            Sums(ways, line, inner // (2 * line), width, DOWN_SHARES, plan_down, False, "back"),
+            Sums(ways, line, rows, inner, UP_SHARES, plan_up),
+            Sums(ways, line, rows, width, OUT_SHARES, plan_out),
+            Swap(ways, length // ways, width, plan_swap),
+        ],
+    )
+    wide = 6 * HEAD
+    pair_sum = PairSum(
+        line, rows, cols, pairs, (line, rows, wide),
+        lambda i: (pl.ds(0, line), slice(None), pl.ds(pl.multiple_of(i * wide, wide), wide)),
+    )
+    inner_jobs = side.jobs[0].ins() + [remote, remote]
+    return pl.pallas_call(
+        functools.partial(attn_back_kernel, side, pair_sum, math.gcd(length, 256)),
+        grid=(2 * pairs,),
+        in_specs=[
+            pl.BlockSpec((length, block), lambda i: (0, first(i))),
+            pl.BlockSpec((width, block), lambda i: (0, first(i))),
+            remote,
+            remote,
+            whole((8, width)),
+            whole((width, length)),
+            remote,
+            pl.BlockSpec((wide, length), lambda i: (second(i), 0)),
+            pl.BlockSpec((None, 8, length), lambda i: (second(i), 0, 0)),
+            pl.BlockSpec((wide, width), lambda i: (second(i), 0)),
+            whole((width, length)),
+            remote,
+        ]
+        + inner_jobs,
+        out_specs=[pair_sum.out()[0], square, whole((1, width)), whole((1, width))] + side.out_specs(),
+        out_shape=[
+            pair_sum.out()[1],
+            jax.ShapeDtypeStruct((length, width), BF16),
+            jax.ShapeDtypeStruct((1, width), F32),
+            jax.ShapeDtypeStruct((1, width), F32),
+        ]
+        + side.out_shape(),
+        scratch_shapes=[
+            pltpu.VMEM((length, width), F32),
+            pltpu.VMEM((length, width), F32),
+            pltpu.VMEM((width, length), BF16),
+            pltpu.VMEM((length, width), BF16),
+            pltpu.VMEM((line, 2, rows, width), BF16),
+            pltpu.SemaphoreType.DMA((4,)),
+        ]
+        + pair_sum.scratch()
+        + side.scratch(),
+        compiler_params=remote_params(3),
+        name="attn_back",
+    )(gu, w_up, hidden, gout, own_rows, mixed, w_out, packed, aux, w_qkv, ready, x, *carried, grad_up, out)
+
+
+def tail_kernel(side, *refs):
+    jobs = len(side.jobs)
+    side.bind([[ref] for ref in refs[:jobs]], refs[jobs : 2 * jobs], refs[2 * jobs :])
+    side.place.hail()
+    side.place.greet()
+    for n in range(12):
+        side.at(0, n)
+        side.at(0, ("after", n))
+
+
+def tail(ways, line, sums, pieces):
+    plan = {n: (0, n) for n in range(12)}
+    jobs = [Sums(ways, line, v.shape[-2], v.shape[-1], shares, plan, paired) for v, shares, paired in sums]
+    side = Side(ways, line, jobs + [Swap(ways, pieces.shape[1], pieces.shape[2], {0: (0, ("after", 1)), 1: (0, ("after", 3)), 2: (0, 11)})])
+    arrays = [v for v, _, _ in sums] + [pieces]
+    return pl.pallas_call(
+        functools.partial(tail_kernel, side),
+        in_specs=[pl.BlockSpec(memory_space=pl.ANY)] * len(arrays),
+        out_specs=side.out_specs(),
+        out_shape=side.out_shape(),
+        scratch_shapes=side.scratch(),
+        compiler_params=remote_params(4),
+        name="tail",
+    )(*arrays)
+
+
+def finish_kernel(groups, *refs):
+    refs = list(refs)
+    sources = [[refs.pop(0) for _ in range(many)] for many in groups]
+    for parts, target in zip(sources, refs):
+        at = 0
+        for part in parts:
+            cols = part.shape[-1]
+            target[..., at : at + cols] = part[...].astype(target.dtype)
+            at += cols
+
+
+def finish(groups, kinds, steps):
+    arrays = [v for group in groups for v in group]
+    wholes = [
+        jax.ShapeDtypeStruct(group[0].shape[:-1] + (sum(v.shape[-1] for v in group),), kind)
+        for group, kind in zip(groups, kinds)
+    ]
+
+    def spec(v):
+        block = (v.shape[0] // steps,) + v.shape[1:]
+        zeros = (0,) * (v.ndim - 1)
+        return pl.BlockSpec(block, lambda i: (i,) + zeros)
+
+    return pl.pallas_call(
+        functools.partial(finish_kernel, [len(group) for group in groups]),
+        grid=(steps,),
+        in_specs=[spec(v) for v in arrays],
+        out_specs=[spec(v) for v in wholes],
+        out_shape=wholes,
+        compiler_params=params(),
+        name="finish",
+    )(*arrays)
+
+
+def exchange(pieces, me, ways):
+    return [pieces[0]] + [
+        lax.ppermute(pieces[k], "seq", [(s, s ^ k) for s in range(ways)]) for k in range(1, ways)
+    ]
+
+
+def by_partner(slots, me, ways):
+    return [lax.dynamic_index_in_dim(slots, me ^ k, 0, keepdims=False) for k in range(ways)]
+
+
+def body(tokens, cotangent, bins, live_count, w_qkv, w_out, w_up, w_down, gain_attn, gain_mlp):
+    slots, rows, width = tokens.shape
+    ways = lax.axis_size("seq")
+    batch_ways = lax.axis_size("batch")
+    line = batch_ways // 2
+    me = lax.axis_index("seq")
+    x, ready_attn, packed, w_turned, own_rows = entry(bins, live_count, tokens, gain_attn, gain_mlp, w_qkv)
+    packed, later = lax.optimization_barrier((packed, cotangent))
+    cots = exchange(by_partner(later, me, ways), me, ways)
+    mixed, aux = attend(packed)
+    hidden, ready_mlp, gout, act, slope, grad_down = mlp(x, mixed, w_out, own_rows, cots, w_up)
+
+    def blocks(v):
+        return v.reshape(line, 2, v.shape[0] // batch_ways, v.shape[1])
+
+    out, grad_upward, grad_up, *carried = mlp_back(
+        gout, act, slope, w_down, ready_mlp, hidden, blocks(grad_down), ways
+    )
+    qkv_pair, grad_x, row_attn, row_mlp, sum_down, sum_up, sum_out, output = attn_back(
+        grad_upward, w_up, hidden, gout, own_rows, mixed, w_out, packed, aux, w_turned, ready_attn, x,
+        carried, blocks(grad_up), out.reshape(ways, rows, width), ways,
+    )
+    own_bin = lax.dynamic_index_in_dim(bins, me, 0)
+    onehot = (jnp.arange(gain_attn.shape[0], dtype=jnp.int32) == own_bin[0]).astype(F32)[:, None]
+    bins_here = gain_attn.shape[0] // batch_ways
+    tables = jnp.concatenate(
+        [(onehot * v).reshape(batch_ways, bins_here, width) for v in (row_attn, row_mlp)], axis=1
+    )
+    tables = tables.astype(BF16).reshape(line, 2, 32, -1)
+    sum_qkv, sum_tables, grad_tokens = tail(
+        ways,
+        line,
+        [(qkv_pair, QKV_SHARES, True), (tables, (0,), False)],
+        grad_x.reshape(ways, rows, width),
+    )
+    sum_tables = sum_tables.reshape(2 * bins_here, width)
+    fine = (2 * ways, slots * rows // (2 * ways), width)
+    output, grad_tokens, *sums = finish(
+        (
+            [output.reshape(fine)],
+            [grad_tokens.reshape(fine)],
+            [sum_qkv],
+            [sum_out],
+            [sum_up],
+            [sum_down],
+        ),
+        (BF16,) + (F32,) * 5,
+        2 * ways,
+    )
+    return (
+        output.reshape(tokens.shape),
+        grad_tokens.reshape(tokens.shape),
+        *sums,
+        sum_tables[:bins_here].astype(F32),
+        sum_tables[bins_here:].astype(F32),
+    )
+
+
+def plain_norm(values_in):
     centred = values_in - jnp.mean(values_in, axis=-1, keepdims=True)
     inverse = lax.rsqrt(jnp.mean(centred * centred, axis=-1, keepdims=True) + 1e-05)
     return (centred * inverse, inverse)
 
 
-def norm_back(grad_normed, normed, inverse):
+def plain_norm_back(grad_normed, normed, inverse):
     first_mean = jnp.mean(grad_normed, axis=-1, keepdims=True)
     second_mean = jnp.mean(grad_normed * normed, axis=-1, keepdims=True)
     return inverse * (grad_normed - first_mean - normed * second_mean)
 
 
-def weight_grad(left, right):
+def plain_weight_grad(left, right):
     return lax.dot_general(
         left, right, (((0,), (0,)), ((), ())), preferred_element_type=jnp.float32
     )
 
 
-def split_heads(packed, heads_here):
+def plain_heads(packed, heads_here):
     shaped = packed.reshape(packed.shape[0], heads_here, 3, -1)
     return (shaped[:, :, 0], shaped[:, :, 1], shaped[:, :, 2])
 
 
-def attend_one(packed, heads_here, block_rows):
-    queries, key_rows, values = split_heads(packed, heads_here)
+def plain_attend(packed, heads_here, block_rows):
+    queries, key_rows, values = plain_heads(packed, heads_here)
     length, head_size = (queries.shape[0], queries.shape[2])
     factor = head_size ** (-0.5)
     blocked = queries.reshape(length // block_rows, block_rows, heads_here, head_size)
@@ -57,8 +1335,8 @@
     return (mixed_rows.reshape(length, heads_here * head_size), logsum)
 
 
-def attend_back(packed, logsum, grad_mixed, heads_here, block_rows):
-    queries, key_rows, values = split_heads(packed, heads_here)
+def plain_attend_back(packed, logsum, grad_mixed, heads_here, block_rows):
+    queries, key_rows, values = plain_heads(packed, heads_here)
     length, head_size = (queries.shape[0], queries.shape[2])
     factor = head_size ** (-0.5)
     count_blocks = length // block_rows
@@ -105,7 +1383,7 @@
     return stacked.reshape(length, heads_here * 3 * head_size).astype(jnp.bfloat16)
 
 
-def body(tokens, cotangent, bins, live_count, w_qkv, w_out, w_up, w_down, gain_attn, gain_mlp):
+def plain_body(tokens, cotangent, bins, live_count, w_qkv, w_out, w_up, w_down, gain_attn, gain_mlp):
     slot_count, local_rows, model_width = tokens.shape
     seq_ways = lax.axis_size("seq")
     heads_here = HEADS // seq_ways
@@ -119,13 +1397,13 @@
     inputs = tokens.astype(jnp.float32)
 
     def attention_part():
-        normed_attn, inverse_attn = layer_norm(inputs)
+        normed_attn, inverse_attn = plain_norm(inputs)
         ready_attn = (normed_attn * gains_attn).astype(jnp.bfloat16).reshape(row_count, model_width)
         packed = jnp.dot(ready_attn, w_qkv, preferred_element_type=jnp.float32).astype(jnp.bfloat16)
         packed = packed.reshape(slot_count, local_rows, 3 * model_width)
         item_rows = lax.all_to_all(packed, "seq", split_axis=2, concat_axis=1, tiled=True)
         mixed_items, logsum_items = lax.map(
-            lambda single: attend_one(single, heads_here, block_rows), item_rows
+            lambda single: plain_attend(single, heads_here, block_rows), item_rows
         )
         mixed_rows = lax.all_to_all(
             mixed_items, "seq", split_axis=1, concat_axis=2, tiled=True
@@ -133,7 +1411,7 @@
         return (normed_attn, inverse_attn, ready_attn, item_rows, logsum_items, mixed_rows)
 
     def mlp_part(hidden):
-        normed_mlp, inverse_mlp = layer_norm(hidden)
+        normed_mlp, inverse_mlp = plain_norm(hidden)
         ready_mlp = (normed_mlp * gains_mlp).astype(jnp.bfloat16).reshape(row_count, model_width)
         upward = jnp.dot(ready_mlp, w_up, preferred_element_type=jnp.float32)
         active = jax.nn.gelu(upward).astype(jnp.bfloat16)
@@ -152,40 +1430,40 @@
     alive_mask = (jnp.arange(slot_count, dtype=jnp.int32) < live_count[0]).astype(jnp.float32)
     grad_output = cotangent.astype(jnp.float32) * alive_mask[:, None, None]
     low_output = grad_output.astype(jnp.bfloat16).reshape(row_count, model_width)
-    grad_down = weight_grad(active, low_output)
+    grad_down = plain_weight_grad(active, low_output)
     grad_active = jnp.dot(low_output, w_down.T, preferred_element_type=jnp.float32)
     gelu_values, gelu_pull = jax.vjp(jax.nn.gelu, upward)
     grad_upward = gelu_pull(grad_active)[0].astype(jnp.bfloat16)
-    grad_up = weight_grad(ready_mlp, grad_upward)
+    grad_up = plain_weight_grad(ready_mlp, grad_upward)
     grad_ready_mlp = jnp.dot(grad_upward, w_up.T, preferred_element_type=jnp.float32).reshape(
         slot_count, local_rows, model_width
     )
     table_mlp = jnp.dot(
         onehot.T, jnp.sum(grad_ready_mlp * normed_mlp, axis=1), precision=lax.Precision.HIGHEST
     )
-    grad_hidden = grad_output + norm_back(grad_ready_mlp * gains_mlp, normed_mlp, inverse_mlp)
+    grad_hidden = grad_output + plain_norm_back(grad_ready_mlp * gains_mlp, normed_mlp, inverse_mlp)
     low_hidden = grad_hidden.astype(jnp.bfloat16).reshape(row_count, model_width)
-    grad_out = weight_grad(mixed_rows, low_hidden)
+    grad_out = plain_weight_grad(mixed_rows, low_hidden)
     grad_mixed = jnp.dot(low_hidden, w_out.T, preferred_element_type=jnp.float32).astype(
         jnp.bfloat16
     )
     grad_mixed = grad_mixed.reshape(slot_count, local_rows, model_width)
     grad_mixed_heads = lax.all_to_all(grad_mixed, "seq", split_axis=2, concat_axis=1, tiled=True)
     grad_packed_heads = lax.map(
-        lambda pieces: attend_back(pieces[0], pieces[1], pieces[2], heads_here, block_rows),
+        lambda pieces: plain_attend_back(pieces[0], pieces[1], pieces[2], heads_here, block_rows),
         (packed_heads, logsum, grad_mixed_heads),
     )
     grad_packed = lax.all_to_all(
         grad_packed_heads, "seq", split_axis=1, concat_axis=2, tiled=True
     ).reshape(row_count, 3 * model_width)
-    grad_qkv = weight_grad(ready_attn, grad_packed)
+    grad_qkv = plain_weight_grad(ready_attn, grad_packed)
     grad_ready_attn = jnp.dot(grad_packed, w_qkv.T, preferred_element_type=jnp.float32).reshape(
         slot_count, local_rows, model_width
     )
     table_attn = jnp.dot(
         onehot.T, jnp.sum(grad_ready_attn * normed_attn, axis=1), precision=lax.Precision.HIGHEST
     )
-    grad_tokens = grad_hidden + norm_back(grad_ready_attn * gains_attn, normed_attn, inverse_attn)
+    grad_tokens = grad_hidden + plain_norm_back(grad_ready_attn * gains_attn, normed_attn, inverse_attn)
     gradients = (grad_qkv, grad_out, grad_up, grad_down, table_attn, table_mlp)
     shares = (
         lax.psum_scatter(gradients[0], "batch", scatter_dimension=0, tiled=True),
@@ -219,8 +1497,9 @@
         P(),
         P(),
     )
+    fits = mesh.shape["seq"] == 4 and mesh.shape["batch"] == 8
     return jax.shard_map(
-        body,
+        body if fits else plain_body,
         mesh=mesh,
         in_specs=placed,
         out_specs=(

time: 1330 us -> 337 us (0.25)
  waiting for transfers between devices: 566 us -> 0.01 us
  Pallas kernels: 0 us -> 323 us
  matrix products: 298 us -> 0 us
  local copies, waits for them, and re-layouts: 227 us -> 6.27 us
  other arithmetic: 96.7 us -> 2.2 us
  blocking collectives: 93.5 us -> 0 us
  starting transfers between devices: 19.1 us -> 3.49 us
  between operations: 15.8 us -> 1.64 us
    reduce_scatter x6 -> x0, waiting for transfers between devices: 427 us -> none  [the longest x1 167 us: body(): lax.psum_scatter(gradients[3], 'batch', scatter_dimension=0, tiled=True)]
    pallas_call x0 -> x7, Pallas kernels: none -> 323 us  [the longest x1 123 us: attn_back(): pl.pallas_call(functools.partial(attn_back_kernel, side, pair_sum, math.g...]
    dot_general x88 -> x0, matrix products: 298 us -> none  [the longest x24 58 us: per_block(): jnp.einsum('qhd,khd->hqk', query_block, key_rows, preferred_element_type=...]
    all_to_all x1 -> x0, blocking collectives: 76.8 us -> none  [body(): lax.all_to_all(grad_packed_heads, 'seq', split_axis=1, concat_axis=2, til...]
    psum x1 -> x0, waiting for transfers between devices: 71.3 us -> none  [body(): lax.psum(shares[0].astype(jnp.bfloat16), 'seq').astype(jnp.float32)]
    all_to_all x4 -> x0, waiting for transfers between devices: 67.3 us -> none  [the longest x1 51.6 us: attention_part(): lax.all_to_all(packed, 'seq', split_axis=2, concat_axis=1, tiled=True)]
    all_to_all x7 -> x0, local copies, waits for them, and re-layouts: 47.2 us -> none  [the longest x2 21.3 us: attention_part(): lax.all_to_all(packed, 'seq', split_axis=2, concat_axis=1, tiled=True)]
    convert_element_type x25 -> x2, other arithmetic: 48.1 us -> 1.39 us  [the longest x1 0.74 us: body(): sum_tables[bins_here:].astype(F32)]
  transfers between devices with their start and end apart: 11 -> 3, of which waited for: 8 -> 0; matrix products, arithmetic and copies ran while one was open for 35% -> 0% of each run, Pallas kernels for 0% -> 6%
where the time goes in v2:
time: 337 us
  Pallas kernels  323 us (96%)
  local copies, waits for them, and re-layouts  6.27 us (2%)
  starting transfers between devices  3.49 us (1%)
    pallas_call x1, Pallas kernels, attn_back(): pl.pallas_call(functools.partial(attn_back_kernel, side, pair_sum, math.g...  123 us
    pallas_call x1, Pallas kernels, tail(): pl.pallas_call(functools.partial(tail_kernel, side), in_specs=[pl.BlockSp...  56.1 us
    pallas_call x1, Pallas kernels, mlp_back(): pl.pallas_call(functools.partial(mlp_back_kernel, side), grid=(8,), in_sp...  49.4 us
    pallas_call x1, Pallas kernels, entry(): pl.pallas_call(functools.partial(entry_kernel, ways, math.gcd(cols, 1024)...  33.3 us
    pallas_call x1, Pallas kernels, mlp(): pl.pallas_call(functools.partial(mlp_kernel, len(cots)), grid=(inner // b...  31.2 us
    pallas_call x1, Pallas kernels, attend(): pl.pallas_call(functools.partial(attend_kernel, bq=math.gcd(length, 256))...  21.4 us
    pallas_call x1, Pallas kernels, finish(): pl.pallas_call(functools.partial(finish_kernel, [len(group) for group in...  9.18 us
  transfers between devices with their start and end apart: 3, of which 0 were waited for; matrix products, arithmetic and copies ran while one was open for 0% of the time, Pallas kernels for 6%

profile of v2, /device:TPU:0, one launch (start us, length us, event | category | flops | bytes accessed | tf_op | source)
XLA Modules:
  0.0 337.0 jit_solution(9628996016105764363)
XLA Ops:
  1.3 33.3 %entry.1 = (bf16[1024,1024]{1,0:T(8,128)(2,1)}, bf16[1024,1024]{1,0:T(8,128)(2,1)}, bf16[3072,1024]{1,0:T(8,128)(2,1)}, bf16[3072,1024]{1,0:T(8,128)(2,1)}, f32[8,1024]{1,0:T(8,128)}) custom-call(s32[4]{0:T(128)} %refs_0_.1, s32[1]{0:T(128)S(6)} %copy.18.refs_1_, bf16[4,256,1024]{2,1,0:T(8,128)(2,1)} %refs_2_.2, f32[64,1024]{1,0:T(8,128)} %refs_3_.2, ...), custom_call_target="tpu_custom_call" | custom-call | tf_op jit(solution)/shard_map/entry/pallas_call | solution.py:137
  34.6 0.0 copy-start.1
  34.6 2.9 dynamic-slice_bitcast_fusion
  37.5 1.5 collective-permute-start
  38.9 1.5 collective-permute-start.1
  40.4 0.5 collective-permute-start.2
  41.0 0.0 copy-done.1
  41.0 0.6 dynamic_slice.21
  41.6 21.4 %attend.1 = (bf16[1024,1024]{1,0:T(8,128)(2,1)}, f32[8,8,1024]{2,1,0:T(8,128)}) custom-call(bf16[3072,1024]{1,0:T(8,128)(2,1)} %get-tuple-element.47.p_ref.refs_7_), custom_call_target="tpu_custom_call" | custom-call | tf_op jit(solution)/shard_map/attend/pallas_call | solution.py:246
  63.0 0.7 fusion
  63.6 0.0 collective-permute-done.refs_5_
  63.6 0.0 copy-start
  63.6 0.0 collective-permute-done.1.refs_6_
  63.6 0.0 collective-permute-done.2.refs_7_
  63.7 0.8 copy-done
  64.4 31.2 %mlp.1 = (f32[1024,1024]{1,0:T(8,128)}, bf16[1024,1024]{1,0:T(8,128)(2,1)}, bf16[1024,1024]{1,0:T(8,128)(2,1)}, bf16[1024,4096]{1,0:T(8,128)(2,1)}, bf16[1024,40...) custom-call(bf16[1024,1024]{1,0:T(8,128)(2,1)} %get-tuple-element.45.refs_0_.refs_11_, ...), custom_call_target="tpu_custom_call" | custom-call | tf_op jit(solution)/shard_map/mlp/pallas_call | solution.py:910
  95.6 49.4 %mlp_back.1 = (bf16[1024,1024]{1,0:T(8,128)(2,1)}, bf16[1024,4096]{1,0:T(8,128)(2,1)}, bf16[1024,4096]{1,0:T(8,128)(2,1)}, bf16[192,1024]{1,0:T(8,128)(2,1)}, bf16[4,320,256]{2,1,0:T(8,128)(2,1)}) custom-call(bf16[1024,1024]{1,0:T(8,128)(2,1)} %get-tuple-element.51.refs_0_.refs_3_, bf16[1024,4096]{1,0:T(8,128)(2,1)} %get-tuple-element.52.refs_1_, ...), custom_call_target="tpu_custom_call" | custom-call | tf_op jit(solution)/shard_map/mlp_back/pallas_call | solution.py:972
  145.0 122.9 %attn_back.1 = (bf16[4,128,3072]{2,1,0:T(8,128)(2,1)}, bf16[1024,1024]{1,0:T(8,128)(2,1)}, f32[1,1024]{1,0:T(1,128)}, f32[1,1024]{1,0:T(1,128)}, bf16[512,1024]{...) custom-call(bf16[1024,4096]{1,0:T(8,128)(2,1)} %get-tuple-element.57.refs_0_,, ...), custom_call_target="tpu_custom_call" | custom-call | tf_op jit(solution)/shard_map/attn_back/pallas_call | solution.py:1120
  267.9 0.8 multiply_convert_fusion.1
  268.7 0.8 convert_element_type.25.refs_1_
  269.5 56.1 %tail.1 = (bf16[128,3072]{1,0:T(8,128)(2,1)}, bf16[32,512]{1,0:T(8,128)(2,1)}, bf16[4,256,1024]{2,1,0:T(8,128)(2,1)}) custom-call(bf16[4,128,3072]{2,1,0:T(8,128)(2,1)} %get-tuple-element.66.refs_0_, bf16[4,2,32,512]{3,2,1,0:T(8,128)(2,1)} %convert_element_type.25.refs_1_, bf16[4,256,1024]{2,1,0:T(8,128)(2,1)} %bitcast.24), custom_call_target="tpu_custom_call" | custom-call | tf_op jit(solution)/shard_map/tail/pallas_call | solution.py:1176
  325.6 0.7 slice_convert_fusion
  326.3 0.6 reshape.85
  326.9 0.6 reshape.86
  327.6 9.2 %finish.1 = (bf16[8,128,1024]{2,1,0:T(8,128)(2,1)}, f32[8,128,1024]{2,1,0:T(8,128)}, f32[128,3072]{1,0:T(8,128)}, f32[128,1024]{1,0:T(8,128)}, f32[128,4096]{1,0:T(8,128)}, /*index=5*/f32[512,1024]{1,0:T(8,128)}) custom-call(bf16[8,128,1024]{2,1,0:T(8,128)(2,1)} %bitcast.21, bf16[8,128,1024]{2,1,0:T(8,128)(2,1)} %bitcast.23, ...), custom_call_target="tpu_custom_call" | custom-call | tf_op jit(solution)/shard_map/finish/pallas_call | solution.py:1210
  (1 shorter events, 0.0 us)
Async XLA Ops:
  34.6 6.4 %copy-start.1 = (s32[4]{0:T(128)S(1)}, s32[4]{0:T(128)}, u32[]{:S(2)}) copy-start(s32[4]{0:T(128)} %refs_0_.1) | copy-start | bytes 52
  37.5 26.1 %collective-permute-start = (bf16[256,1024]{1,0:T(8,128)(2,1)}, bf16[256,1024]{1,0:T(8,128)(2,1)S(1)}, u32[]{:S(2)}, u32[]{:S(2)}) collective-permute-start(bf16[256,1024]{1,0:T(8,128)(2,1)} %get-tuple-element.84), channel_id=1, source_target_pairs={{0,8},{8,0},{16,24},{24,16},{1,9},{9,1},{17,25},{25,17},{2,10},{10... | collective-permute-start | bytes 1572872 | tf_op jit(solution)/shard_map/ppermute | solution.py:1223
  38.9 24.7 %collective-permute-start.1 = (bf16[256,1024]{1,0:T(8,128)(2,1)}, bf16[256,1024]{1,0:T(8,128)(2,1)}, u32[]{:S(2)}, u32[]{:S(2)}) collective-permute-start(bf16[256,1024]{1,0:T(8,128)(2,1)} %get-tuple-element.83), channel_id=1, source_target_pairs={{0,16},{8,24},{16,0},{24,8},{1,17},{9,25},{17,1},{25,9},{2,18},{10... | collective-permute-start | bytes 1572872 | tf_op jit(solution)/shard_map/ppermute | solution.py:1223
  40.4 23.2 %collective-permute-start.2 = (bf16[256,1024]{1,0:T(8,128)(2,1)}, bf16[256,1024]{1,0:T(8,128)(2,1)}, u32[]{:S(2)}, u32[]{:S(2)}) collective-permute-start(bf16[256,1024]{1,0:T(8,128)(2,1)} %get-tuple-element.82), channel_id=1, source_target_pairs={{0,24},{8,16},{16,8},{24,0},{1,25},{9,17},{17,9},{25,1},{2,26},{10... | collective-permute-start | bytes 1572872 | tf_op jit(solution)/shard_map/ppermute | solution.py:1223
  63.6 0.8 copy-start

commit v3 on v2

--- a/solution.py
+++ b/solution.py
@@ -16,7 +16,7 @@
 GELU_C = math.sqrt(2 / math.pi)
 GELU_K = 0.044715
 VMEM = 63 * 2**20
-DOWN_SHARES = (0.65,)
+DOWN_SHARES = (0.75,)
 UP_SHARES = (0.5,)
 OUT_SHARES = (0.5,)
 QKV_SHARES = (0.5, 0.25)
@@ -967,7 +967,7 @@
     block = inner // 8
     cols = pl.BlockSpec((length, block), lambda i: (0, i))
     square = whole((length, width))
-    plan = {0: (0, 0), 1: (2, 0), 2: (4, 1), 3: (7, 0), 4: (7, "end")}
+    plan = {0: (0, 0), 1: (2, 0), 2: (3, 1), 3: (6, 0), 4: (7, "end")}
     side = Side(ways, line, [Sums(ways, line, down_rows, width, DOWN_SHARES, plan, False, "front")])
     return pl.pallas_call(
         functools.partial(mlp_back_kernel, side),
@@ -995,20 +995,22 @@
 
 
 def attn_back_kernel(side, pair_sum, bq, *refs):
+    bins, *refs = refs
     gu, w_up, hidden, gout, own_rows, mixed, w_out, packed, aux, w_qkv, ready, x = refs[:12]
     back_from = len(side.jobs[0].ins())
     carried, source_up, source_out = refs[12 : 12 + back_from], refs[12 + back_from], refs[13 + back_from]
     refs = refs[14 + back_from :]
-    grad_qkv, grad_x, table_attn, table_mlp = refs[:4]
+    grad_qkv, grad_x, tables = refs[:3]
     many = len(side.out_shape())
-    finals, refs = refs[4 : 4 + many], refs[4 + many :]
-    back_sum, grad_hidden, grad_mixed, spare, grad_out, late = refs[:6]
+    finals, refs = refs[3 : 3 + many], refs[3 + many :]
+    back_sum, grad_hidden, grad_mixed, spare, grad_out, row_mlp, late = refs[:7]
     pairing = len(pair_sum.scratch())
-    side.bind([carried, [source_up], [grad_out], [source_out]], finals, refs[6 + pairing :])
-    pair_sum.bind(side.place, grad_qkv, refs[6 : 6 + pairing])
+    side.bind([carried, [source_up], [grad_out], [source_out]], finals, refs[7 + pairing :])
+    pair_sum.bind(side.place, grad_qkv, refs[7 : 7 + pairing])
     i = pl.program_id(0)
     steps = pl.num_programs(0) // 2
     length, width = gout.shape
+    line = grad_out.shape[0]
     span = math.gcd(length, 256)
     load_hidden = pltpu.make_async_copy(hidden, grad_hidden, late.at[0])
     load_w = pltpu.make_async_copy(w_out, spare, late.at[1])
@@ -1042,7 +1044,7 @@
             g = back_sum[here]
             total = total + jnp.sum(g * normed, axis=0, keepdims=True)
             grad_hidden[here] = grad_x[here].astype(F32) + norm_back(g * own_rows[1:2], normed, inverse)
-        table_mlp[...] = total
+        row_mlp[...] = total
         side.at(i, "norm")
         low = grad_hidden[...].astype(BF16)
         grad_mixed[...] = nt(spare[...], low).astype(BF16)
@@ -1075,12 +1077,19 @@
             g = back_sum[here]
             total = total + jnp.sum(g * normed, axis=0, keepdims=True)
             grad_x[here] = (grad_hidden[here] + norm_back(g * own_rows[0:1], normed, inverse)).astype(BF16)
-        table_attn[...] = total
+        bins_here = tables.shape[2] // 4
+        marked = lax.broadcasted_iota(jnp.int32, (2 * line * bins_here, width), 0) == bins[side.place.me]
+        both = [jnp.where(marked, row, 0.0) for row in (total, row_mlp[...])]
+        half = width // 2
+        for b in range(2 * line):
+            own = slice(b * bins_here, (b + 1) * bins_here)
+            parts = [v[own, cut] for cut in (slice(0, half), slice(half, width)) for v in both]
+            tables[b // 2, b % 2] = jnp.concatenate(parts, axis=0).astype(BF16)
         pair_sum.take_rest(i - steps)
         side.at(i, "end")
 
 
-def attn_back(gu, w_up, hidden, gout, own_rows, mixed, w_out, packed, aux, w_qkv, ready, x, carried, grad_up, out, ways):
+def attn_back(bins, gu, w_up, hidden, gout, own_rows, mixed, w_out, packed, aux, w_qkv, ready, x, carried, grad_up, out, ways):
     length, width = gout.shape
     inner = w_up.shape[1]
     cols = packed.shape[0]
@@ -1121,6 +1130,7 @@
         functools.partial(attn_back_kernel, side, pair_sum, math.gcd(length, 256)),
         grid=(2 * pairs,),
         in_specs=[
+            pl.BlockSpec(memory_space=pltpu.SMEM),
             pl.BlockSpec((length, block), lambda i: (0, first(i))),
             pl.BlockSpec((width, block), lambda i: (0, first(i))),
             remote,
@@ -1135,12 +1145,11 @@
             remote,
         ]
         + inner_jobs,
-        out_specs=[pair_sum.out()[0], square, whole((1, width)), whole((1, width))] + side.out_specs(),
+        out_specs=[pair_sum.out()[0], square, whole((line, 2, 32, width // 2))] + side.out_specs(),
         out_shape=[
             pair_sum.out()[1],
             jax.ShapeDtypeStruct((length, width), BF16),
-            jax.ShapeDtypeStruct((1, width), F32),
-            jax.ShapeDtypeStruct((1, width), F32),
+            jax.ShapeDtypeStruct((line, 2, 32, width // 2), BF16),
         ]
         + side.out_shape(),
         scratch_shapes=[
@@ -1149,13 +1158,14 @@
             pltpu.VMEM((width, length), BF16),
             pltpu.VMEM((length, width), BF16),
             pltpu.VMEM((line, 2, rows, width), BF16),
+            pltpu.VMEM((1, width), F32),
             pltpu.SemaphoreType.DMA((4,)),
         ]
         + pair_sum.scratch()
         + side.scratch(),
         compiler_params=remote_params(3),
         name="attn_back",
-    )(gu, w_up, hidden, gout, own_rows, mixed, w_out, packed, aux, w_qkv, ready, x, *carried, grad_up, out)
+    )(bins, gu, w_up, hidden, gout, own_rows, mixed, w_out, packed, aux, w_qkv, ready, x, *carried, grad_up, out)
 
 
 def tail_kernel(side, *refs):
@@ -1170,7 +1180,11 @@
 
 def tail(ways, line, sums, pieces):
     plan = {n: (0, n) for n in range(12)}
-    jobs = [Sums(ways, line, v.shape[-2], v.shape[-1], shares, plan, paired) for v, shares, paired in sums]
+    behind = {n: (0, ("after", n)) for n in range(12)}
+    jobs = [
+        Sums(ways, line, v.shape[-2], v.shape[-1], shares, plan if paired else behind, paired)
+        for v, shares, paired in sums
+    ]
     side = Side(ways, line, jobs + [Swap(ways, pieces.shape[1], pieces.shape[2], {0: (0, ("after", 1)), 1: (0, ("after", 3)), 2: (0, 11)})])
     arrays = [v for v, _, _ in sums] + [pieces]
     return pl.pallas_call(
@@ -1184,38 +1198,71 @@
     )(*arrays)
 
 
-def finish_kernel(groups, *refs):
-    refs = list(refs)
-    sources = [[refs.pop(0) for _ in range(many)] for many in groups]
-    for parts, target in zip(sources, refs):
-        at = 0
-        for part in parts:
-            cols = part.shape[-1]
-            target[..., at : at + cols] = part[...].astype(target.dtype)
-            at += cols
-
-
-def finish(groups, kinds, steps):
-    arrays = [v for group in groups for v in group]
-    wholes = [
-        jax.ShapeDtypeStruct(group[0].shape[:-1] + (sum(v.shape[-1] for v in group),), kind)
-        for group, kind in zip(groups, kinds)
-    ]
-
-    def spec(v):
-        block = (v.shape[0] // steps,) + v.shape[1:]
-        zeros = (0,) * (v.ndim - 1)
-        return pl.BlockSpec(block, lambda i: (i,) + zeros)
-
+def finish_kernel(many, *refs):
+    tables, refs = refs[0], refs[1:]
+    sources, refs = refs[:many], refs[many:]
+    table_attn, table_mlp = refs[:2]
+    targets, refs = refs[2 : 2 + many], refs[2 + many :]
+    low, wide, (came, left) = refs[:many], refs[many : 2 * many], refs[2 * many :]
+    parts = 4
+
+    def span(n, part):
+        rows = low[n].shape[0] // parts
+        return pl.ds(part * rows, rows)
+
+    def load(n, part):
+        at = span(n, part)
+        return pltpu.make_async_copy(sources[n].at[at], low[n].at[at], came.at[n, part])
+
+    def store(n, part):
+        at = span(n, part)
+        return pltpu.make_async_copy((wide[n] if changed(n) else low[n]).at[at], targets[n].at[at], left.at[n, part])
+
+    def changed(n):
+        return targets[n].dtype != low[n].dtype
+
+    pieces = [(n, part) for n in range(many) for part in range(parts)]
+    for piece in pieces:
+        load(*piece).start()
+    half = tables.shape[1]
+    for first, table in ((0, table_attn), (8, table_mlp)):
+        table[:, :half] = tables[first : first + 8].astype(F32)
+        table[:, half:] = tables[first + 16 : first + 24].astype(F32)
+    for n, part in pieces:
+        load(n, part).wait()
+        if not changed(n):
+            store(n, part).start()
+            continue
+        rows, cols = low[n].shape[0] // parts, low[n].shape[1]
+        step = row_step(rows, cols)
+
+        def one(r, carry, n=n, part=part, rows=rows, step=step):
+            at = pl.ds(pl.multiple_of(part * rows + r * step, step), step)
+            wide[n][at] = low[n][at].astype(F32)
+            return carry
+
+        lax.fori_loop(0, rows // step, one, 0)
+        store(n, part).start()
+    for piece in pieces:
+        store(*piece).wait()
+
+
+def finish(tables, arrays, kinds):
+    many = len(arrays)
+    remote = pl.BlockSpec(memory_space=pl.ANY)
+    here = pl.BlockSpec(memory_space=pltpu.VMEM)
+    table = jax.ShapeDtypeStruct((8, 2 * tables.shape[1]), F32)
     return pl.pallas_call(
-        functools.partial(finish_kernel, [len(group) for group in groups]),
-        grid=(steps,),
-        in_specs=[spec(v) for v in arrays],
-        out_specs=[spec(v) for v in wholes],
-        out_shape=wholes,
+        functools.partial(finish_kernel, many),
+        in_specs=[here] + [remote] * many,
+        out_specs=[here, here] + [remote] * many,
+        out_shape=[table, table] + [jax.ShapeDtypeStruct(v.shape, kind) for v, kind in zip(arrays, kinds)],
+        scratch_shapes=[pltpu.VMEM(v.shape, BF16) for v in arrays]
+        + [pltpu.VMEM(v.shape, F32) for v in arrays]
+        + [pltpu.SemaphoreType.DMA((many, 4))] * 2,
         compiler_params=params(),
         name="finish",
-    )(*arrays)
+    )(tables, *arrays)
 
 
 def exchange(pieces, me, ways):
@@ -1246,44 +1293,19 @@
     out, grad_upward, grad_up, *carried = mlp_back(
         gout, act, slope, w_down, ready_mlp, hidden, blocks(grad_down), ways
     )
-    qkv_pair, grad_x, row_attn, row_mlp, sum_down, sum_up, sum_out, output = attn_back(
-        grad_upward, w_up, hidden, gout, own_rows, mixed, w_out, packed, aux, w_turned, ready_attn, x,
+    qkv_pair, grad_x, tables, sum_down, sum_up, sum_out, output = attn_back(
+        bins, grad_upward, w_up, hidden, gout, own_rows, mixed, w_out, packed, aux, w_turned, ready_attn, x,
         carried, blocks(grad_up), out.reshape(ways, rows, width), ways,
     )
-    own_bin = lax.dynamic_index_in_dim(bins, me, 0)
-    onehot = (jnp.arange(gain_attn.shape[0], dtype=jnp.int32) == own_bin[0]).astype(F32)[:, None]
-    bins_here = gain_attn.shape[0] // batch_ways
-    tables = jnp.concatenate(
-        [(onehot * v).reshape(batch_ways, bins_here, width) for v in (row_attn, row_mlp)], axis=1
-    )
-    tables = tables.astype(BF16).reshape(line, 2, 32, -1)
     sum_qkv, sum_tables, grad_tokens = tail(
         ways,
         line,
         [(qkv_pair, QKV_SHARES, True), (tables, (0,), False)],
         grad_x.reshape(ways, rows, width),
     )
-    sum_tables = sum_tables.reshape(2 * bins_here, width)
-    fine = (2 * ways, slots * rows // (2 * ways), width)
-    output, grad_tokens, *sums = finish(
-        (
-            [output.reshape(fine)],
-            [grad_tokens.reshape(fine)],
-            [sum_qkv],
-            [sum_out],
-            [sum_up],
-            [sum_down],
-        ),
-        (BF16,) + (F32,) * 5,
-        2 * ways,
-    )
-    return (
-        output.reshape(tokens.shape),
-        grad_tokens.reshape(tokens.shape),
-        *sums,
-        sum_tables[:bins_here].astype(F32),
-        sum_tables[bins_here:].astype(F32),
-    )
+    arrays = [v.reshape(slots * rows, width) for v in (grad_tokens, output)] + [sum_qkv, sum_out, sum_up, sum_down]
+    sum_attn, sum_mlp, grad_tokens, output, *sums = finish(sum_tables, arrays, [F32, BF16] + [F32] * 4)
+    return (output.reshape(tokens.shape), grad_tokens.reshape(tokens.shape), *sums, sum_attn, sum_mlp)
 
 
 def plain_norm(values_in):

time: 337 us -> 331 us (0.982)
  no operation moved by 1% of the time
where the time goes in v3:
time: 331 us
  Pallas kernels  323 us (98%)
  local copies, waits for them, and re-layouts  3.64 us (1%)
  starting transfers between devices  3.49 us (1%)
    pallas_call x1, Pallas kernels, attn_back(): pl.pallas_call(functools.partial(attn_back_kernel, side, pair_sum, math.g...  124 us
    pallas_call x1, Pallas kernels, tail(): pl.pallas_call(functools.partial(tail_kernel, side), in_specs=[pl.BlockSp...  57.4 us
    pallas_call x1, Pallas kernels, mlp_back(): pl.pallas_call(functools.partial(mlp_back_kernel, side), grid=(8,), in_sp...  47.3 us
    pallas_call x1, Pallas kernels, entry(): pl.pallas_call(functools.partial(entry_kernel, ways, math.gcd(cols, 1024)...  33.3 us
    pallas_call x1, Pallas kernels, mlp(): pl.pallas_call(functools.partial(mlp_kernel, len(cots)), grid=(inner // b...  31.2 us
    pallas_call x1, Pallas kernels, attend(): pl.pallas_call(functools.partial(attend_kernel, bq=math.gcd(length, 256))...  21.4 us
    pallas_call x1, Pallas kernels, finish(): pl.pallas_call(functools.partial(finish_kernel, many), in_specs=[here] +...  8.19 us
  transfers between devices with their start and end apart: 3, of which 0 were waited for; matrix products, arithmetic and copies ran while one was open for 0% of the time, Pallas kernels for 6%

profile of v3, /device:TPU:0, one launch (start us, length us, event | category | flops | bytes accessed | tf_op | source)
XLA Modules:
  0.0 331.3 jit_solution(15453270055989994569)
XLA Ops:
  1.3 33.3 %entry.1 = (bf16[1024,1024]{1,0:T(8,128)(2,1)}, bf16[1024,1024]{1,0:T(8,128)(2,1)}, bf16[3072,1024]{1,0:T(8,128)(2,1)}, bf16[3072,1024]{1,0:T(8,128)(2,1)}, f32[8,1024]{1,0:T(8,128)}) custom-call(s32[4]{0:T(128)} %refs_0_.3, s32[1]{0:T(128)S(6)} %copy.18.refs_1_, bf16[4,256,1024]{2,1,0:T(8,128)(2,1)} %refs_2_.3, f32[64,1024]{1,0:T(8,128)} %refs_3_.2, ...), custom_call_target="tpu_custom_call" | custom-call | tf_op jit(solution)/shard_map/entry/pallas_call | solution.py:137
  34.6 2.9 dynamic-slice_bitcast_fusion
  37.4 2.4 collective-permute-start.2
  39.8 0.5 collective-permute-start.1
  40.4 0.6 collective-permute-start
  40.9 21.4 %attend.1 = (bf16[1024,1024]{1,0:T(8,128)(2,1)}, f32[8,8,1024]{2,1,0:T(8,128)}) custom-call(bf16[3072,1024]{1,0:T(8,128)(2,1)} %get-tuple-element.48.p_ref.refs_8_), custom_call_target="tpu_custom_call" | custom-call | tf_op jit(solution)/shard_map/attend/pallas_call | solution.py:246
  62.3 0.0 collective-permute-done.2.refs_7_
  62.3 0.0 copy-start
  62.3 0.0 collective-permute-done.1.refs_6_
  62.4 0.0 collective-permute-done.refs_5_
  62.4 0.8 copy-done
  63.1 31.2 %mlp.1 = (f32[1024,1024]{1,0:T(8,128)}, bf16[1024,1024]{1,0:T(8,128)(2,1)}, bf16[1024,1024]{1,0:T(8,128)(2,1)}, bf16[1024,4096]{1,0:T(8,128)(2,1)}, bf16[1024,40...) custom-call(bf16[1024,1024]{1,0:T(8,128)(2,1)} %get-tuple-element.46.refs_0_.refs_12_, ...), custom_call_target="tpu_custom_call" | custom-call | tf_op jit(solution)/shard_map/mlp/pallas_call | solution.py:910
  94.3 47.3 %mlp_back.1 = (bf16[1024,1024]{1,0:T(8,128)(2,1)}, bf16[1024,4096]{1,0:T(8,128)(2,1)}, bf16[1024,4096]{1,0:T(8,128)(2,1)}, bf16[128,1024]{1,0:T(8,128)(2,1)}, bf16[4,384,256]{2,1,0:T(8,128)(2,1)}) custom-call(bf16[1024,1024]{1,0:T(8,128)(2,1)} %get-tuple-element.52.refs_0_.refs_4_, bf16[1024,4096]{1,0:T(8,128)(2,1)} %get-tuple-element.53.refs_1_, ...), custom_call_target="tpu_custom_call" | custom-call | tf_op jit(solution)/shard_map/mlp_back/pallas_call | solution.py:972
  141.6 123.8 %attn_back.1 = (bf16[4,128,3072]{2,1,0:T(8,128)(2,1)}, bf16[1024,1024]{1,0:T(8,128)(2,1)}, bf16[4,2,32,512]{3,2,1,0:T(8,128)(2,1)}, bf16[512,1024]{1,0:T(8,128)(...) custom-call(s32[4]{0:T(128)} %refs_0_.3, ...), custom_call_target="tpu_custom_call" | custom-call | tf_op jit(solution)/shard_map/attn_back/pallas_call | solution.py:1129
  265.4 57.4 %tail.1 = (bf16[128,3072]{1,0:T(8,128)(2,1)}, bf16[32,512]{1,0:T(8,128)(2,1)}, bf16[4,256,1024]{2,1,0:T(8,128)(2,1)}) custom-call(bf16[4,128,3072]{2,1,0:T(8,128)(2,1)} %get-tuple-element.66.refs_0_, bf16[4,2,32,512]{3,2,1,0:T(8,128)(2,1)} %get-tuple-element.67.refs_1_, bf16[4,256,1024]{2,1,0:T(8,128)(2,1)} %bitcast.21), custom_call_target="tpu_custom_call" | custom-call | tf_op jit(solution)/shard_map/tail/pallas_call | solution.py:1190
  322.8 8.2 %finish.1 = (f32[8,1024]{1,0:T(8,128)}, f32[8,1024]{1,0:T(8,128)}, f32[1024,1024]{1,0:T(8,128)}, bf16[1024,1024]{1,0:T(8,128)(2,1)}, f32[128,3072]{1,0:T(8,128)}...) custom-call(bf16[32,512]{1,0:T(8,128)(2,1)} %get-tuple-element.69.refs_0_, ...), custom_call_target="tpu_custom_call" | custom-call | tf_op jit(solution)/shard_map/finish/pallas_call | solution.py:1255
Async XLA Ops:
  37.4 24.9 %collective-permute-start.2 = (bf16[256,1024]{1,0:T(8,128)(2,1)}, bf16[256,1024]{1,0:T(8,128)(2,1)S(1)}, u32[]{:S(2)}, u32[]{:S(2)}) collective-permute-start(bf16[256,1024]{1,0:T(8,128)(2,1)} %get-tuple-element.84), channel_id=1, source_target_pairs={{0,24},{8,16},{16,8},{24,0},{1,25},{9,17},{17,9},{25,1},{2,26},{10... | collective-permute-start | bytes 1572872 | tf_op jit(solution)/shard_map/ppermute | solution.py:1270
  39.8 22.5 %collective-permute-start.1 = (bf16[256,1024]{1,0:T(8,128)(2,1)}, bf16[256,1024]{1,0:T(8,128)(2,1)}, u32[]{:S(2)}, u32[]{:S(2)}) collective-permute-start(bf16[256,1024]{1,0:T(8,128)(2,1)} %get-tuple-element.85), channel_id=1, source_target_pairs={{0,16},{8,24},{16,0},{24,8},{1,17},{9,25},{17,1},{25,9},{2,18},{10... | collective-permute-start | bytes 1572872 | tf_op jit(solution)/shard_map/ppermute | solution.py:1270
  40.4 22.0 %collective-permute-start = (bf16[256,1024]{1,0:T(8,128)(2,1)}, bf16[256,1024]{1,0:T(8,128)(2,1)}, u32[]{:S(2)}, u32[]{:S(2)}) collective-permute-start(bf16[256,1024]{1,0:T(8,128)(2,1)} %get-tuple-element.86), channel_id=1, source_target_pairs={{0,8},{8,0},{16,24},{24,16},{1,9},{9,1},{17,25},{25,17},{2,10},{10... | collective-permute-start | bytes 1572872 | tf_op jit(solution)/shard_map/ppermute | solution.py:1270
  62.3 0.8 copy-start

commit v4 on v3

--- a/solution.py
+++ b/solution.py
@@ -60,8 +60,10 @@
 
 
 def entry_kernel(ways, steps, *refs):
-    bins, live, tokens, gain_attn, gain_mlp, w, x_out, ready_out, packed_out, w_out, own_rows = refs[:11]
-    here, w_here, w_turned, ready_here, packed_here, send, recv, local, leave = refs[11:]
+    bins, live, tokens, cotangent, gain_attn, gain_mlp, w = refs[:7]
+    x_out, ready_out, packed_out, w_out, own_rows = refs[7:12]
+    cots, refs = refs[12 : 12 + ways], refs[12 + ways :]
+    here, w_here, w_turned, ready_here, packed_here, cots_here, send, recv, local, leave = refs
     place = Place(ways, 0)
     own_bin = bins[place.me]
     gain = gain_attn[pl.ds(own_bin, 1)]
@@ -73,8 +75,10 @@
     cols = w_here.shape[1]
     load_w = pltpu.make_async_copy(w, w_here, local.at[0])
     load_own = pltpu.make_async_copy(tokens.at[place.me], here.at[0], local.at[1])
+    load_cots = pltpu.make_async_copy(cotangent, cots_here, local.at[3])
     load_w.start()
     load_own.start()
+    load_cots.start()
 
     def move(k):
         return pltpu.make_async_remote_copy(
@@ -82,6 +86,9 @@
             send_sem=send.at[k], recv_sem=recv.at[k],
             device_id=place.plane(k), device_id_type=MESH,
         )
+
+    def sort_cots(k):
+        return pltpu.make_async_copy(cots_here.at[place.partner(k)], cots[k], leave.at[3, k])
 
     def span(k):
         return pl.ds(k * rows, rows)
@@ -115,6 +122,9 @@
     save_w = pltpu.make_async_copy(w_turned, w_out, local.at[2])
     save_w.start()
     load_own.wait()
+    load_cots.wait()
+    for k in range(ways):
+        sort_cots(k).start()
     project(0)
     for k in range(1, ways - 1):
         move(k).wait_send()
@@ -125,11 +135,12 @@
     move(ways - 1).wait_send()
     save_w.wait()
     for k in range(ways):
+        sort_cots(k).wait()
         for copy in leaving(k):
             copy.wait()
 
 
-def entry(bins, live, tokens, gain_attn, gain_mlp, w):
+def entry(bins, live, tokens, cotangent, gain_attn, gain_mlp, w):
     ways, rows, width = tokens.shape
     cols = w.shape[1]
     length = ways * rows
@@ -137,31 +148,33 @@
     return pl.pallas_call(
         functools.partial(entry_kernel, ways, math.gcd(cols, 1024)),
         in_specs=[pl.BlockSpec(memory_space=pltpu.SMEM)] * 2
-        + [remote]
+        + [remote] * 2
         + [pl.BlockSpec(memory_space=pltpu.VMEM)] * 2
         + [remote],
-        out_specs=[remote] * 4 + [pl.BlockSpec(memory_space=pltpu.VMEM)],
+        out_specs=[remote] * 4 + [pl.BlockSpec(memory_space=pltpu.VMEM)] + [remote] * ways,
         out_shape=[
             jax.ShapeDtypeStruct((length, width), BF16),
             jax.ShapeDtypeStruct((width, length), BF16),
             jax.ShapeDtypeStruct((cols, length), BF16),
             jax.ShapeDtypeStruct((cols, width), BF16),
             jax.ShapeDtypeStruct((8, width), F32),
-        ],
+        ]
+        + [jax.ShapeDtypeStruct((rows, width), BF16)] * ways,
         scratch_shapes=[
             pltpu.VMEM((ways, rows, width), BF16),
             pltpu.VMEM((width, cols), BF16),
             pltpu.VMEM((cols, width), BF16),
             pltpu.VMEM((ways, width, rows), BF16),
             pltpu.VMEM((ways, cols, rows), BF16),
+            pltpu.VMEM((ways, rows, width), BF16),
             pltpu.SemaphoreType.DMA((ways,)),
             pltpu.SemaphoreType.DMA((ways,)),
-            pltpu.SemaphoreType.DMA((3,)),
-            pltpu.SemaphoreType.DMA((3, ways)),
+            pltpu.SemaphoreType.DMA((4,)),
+            pltpu.SemaphoreType.DMA((4, ways)),
         ],
         compiler_params=pltpu.CompilerParams(vmem_limit_bytes=VMEM, collective_id=0, has_side_effects=True),
         name="entry",
-    )(bins, live, tokens, gain_attn, gain_mlp, w)
+    )(bins, live, tokens, cotangent, gain_attn, gain_mlp, w)
 
 
 def split2(v):
@@ -1281,9 +1294,10 @@
     batch_ways = lax.axis_size("batch")
     line = batch_ways // 2
     me = lax.axis_index("seq")
-    x, ready_attn, packed, w_turned, own_rows = entry(bins, live_count, tokens, gain_attn, gain_mlp, w_qkv)
-    packed, later = lax.optimization_barrier((packed, cotangent))
-    cots = exchange(by_partner(later, me, ways), me, ways)
+    x, ready_attn, packed, w_turned, own_rows, *pieces = entry(
+        bins, live_count, tokens, cotangent, gain_attn, gain_mlp, w_qkv
+    )
+    cots = exchange(pieces, me, ways)
     mixed, aux = attend(packed)
     hidden, ready_mlp, gout, act, slope, grad_down = mlp(x, mixed, w_out, own_rows, cots, w_up)
 

time: 331 us -> 328 us (level)
  transfers between devices with their start and end apart: 3 -> 3, of which waited for: 0 -> 0; matrix products, arithmetic and copies ran while one was open for 0% -> 0% of each run, Pallas kernels for 6% -> 7%
where the time goes in v4:
time: 328 us
  Pallas kernels  323 us (98%)
  starting transfers between devices  3.55 us (1%)
    pallas_call x1, Pallas kernels, attn_back(): pl.pallas_call(functools.partial(attn_back_kernel, side, pair_sum, math.g...  124 us
    pallas_call x1, Pallas kernels, tail(): pl.pallas_call(functools.partial(tail_kernel, side), in_specs=[pl.BlockSp...  57.4 us
    pallas_call x1, Pallas kernels, mlp_back(): pl.pallas_call(functools.partial(mlp_back_kernel, side), grid=(8,), in_sp...  47.2 us
    pallas_call x1, Pallas kernels, entry(): pl.pallas_call(functools.partial(entry_kernel, ways, math.gcd(cols, 1024)...  33.3 us
    pallas_call x1, Pallas kernels, mlp(): pl.pallas_call(functools.partial(mlp_kernel, len(cots)), grid=(inner // b...  31.2 us
    pallas_call x1, Pallas kernels, attend(): pl.pallas_call(functools.partial(attend_kernel, bq=math.gcd(length, 256))...  21.4 us
    pallas_call x1, Pallas kernels, finish(): pl.pallas_call(functools.partial(finish_kernel, many), in_specs=[here] +...  8.19 us
  transfers between devices with their start and end apart: 3, of which 0 were waited for; matrix products, arithmetic and copies ran while one was open for 0% of the time, Pallas kernels for 7%

profile of v4, /device:TPU:0, one launch (start us, length us, event | category | flops | bytes accessed | tf_op | source)
XLA Modules:
  0.0 328.4 jit_solution(2209629225846652732)
XLA Ops:
  1.3 33.3 %entry.1 = (bf16[1024,1024]{1,0:T(8,128)(2,1)}, bf16[1024,1024]{1,0:T(8,128)(2,1)}, bf16[3072,1024]{1,0:T(8,128)(2,1)}, bf16[3072,1024]{1,0:T(8,128)(2,1)}, f32[...) custom-call(s32[4]{0:T(128)} %refs_0_.3, ...), custom_call_target="tpu_custom_call" | custom-call | tf_op jit(solution)/shard_map/entry/pallas_call | solution.py:148
  34.6 1.5 collective-permute-start
  36.1 1.5 collective-permute-start.1
  37.6 0.5 collective-permute-start.2
  38.2 21.4 %attend.1 = (bf16[1024,1024]{1,0:T(8,128)(2,1)}, f32[8,8,1024]{2,1,0:T(8,128)}) custom-call(bf16[3072,1024]{1,0:T(8,128)(2,1)} %get-tuple-element.49.p_ref.refs_8_), custom_call_target="tpu_custom_call" | custom-call | tf_op jit(solution)/shard_map/attend/pallas_call | solution.py:259
  59.6 0.0 collective-permute-done.refs_5_
  59.6 0.0 copy-start
  59.6 0.0 collective-permute-done.1.refs_6_
  59.6 0.0 collective-permute-done.2.refs_7_
  59.6 0.7 copy-done
  60.4 31.2 %mlp.1 = (f32[1024,1024]{1,0:T(8,128)}, bf16[1024,1024]{1,0:T(8,128)(2,1)}, bf16[1024,1024]{1,0:T(8,128)(2,1)}, bf16[1024,4096]{1,0:T(8,128)(2,1)}, bf16[1024,40...) custom-call(bf16[1024,1024]{1,0:T(8,128)(2,1)} %get-tuple-element.48.refs_0_.refs_12_, ...), custom_call_target="tpu_custom_call" | custom-call | tf_op jit(solution)/shard_map/mlp/pallas_call | solution.py:923
  91.5 47.2 %mlp_back.1 = (bf16[1024,1024]{1,0:T(8,128)(2,1)}, bf16[1024,4096]{1,0:T(8,128)(2,1)}, bf16[1024,4096]{1,0:T(8,128)(2,1)}, bf16[128,1024]{1,0:T(8,128)(2,1)}, bf16[4,384,256]{2,1,0:T(8,128)(2,1)}) custom-call(bf16[1024,1024]{1,0:T(8,128)(2,1)} %get-tuple-element.56.refs_0_.refs_4_, bf16[1024,4096]{1,0:T(8,128)(2,1)} %get-tuple-element.57.refs_1_, ...), custom_call_target="tpu_custom_call" | custom-call | tf_op jit(solution)/shard_map/mlp_back/pallas_call | solution.py:985
  138.8 123.8 %attn_back.1 = (bf16[4,128,3072]{2,1,0:T(8,128)(2,1)}, bf16[1024,1024]{1,0:T(8,128)(2,1)}, bf16[4,2,32,512]{3,2,1,0:T(8,128)(2,1)}, bf16[512,1024]{1,0:T(8,128)(...) custom-call(s32[4]{0:T(128)} %refs_0_.3, ...), custom_call_target="tpu_custom_call" | custom-call | tf_op jit(solution)/shard_map/attn_back/pallas_call | solution.py:1142
  262.6 57.4 %tail.1 = (bf16[128,3072]{1,0:T(8,128)(2,1)}, bf16[32,512]{1,0:T(8,128)(2,1)}, bf16[4,256,1024]{2,1,0:T(8,128)(2,1)}) custom-call(bf16[4,128,3072]{2,1,0:T(8,128)(2,1)} %get-tuple-element.70.refs_0_, bf16[4,2,32,512]{3,2,1,0:T(8,128)(2,1)} %get-tuple-element.71.refs_1_, bf16[4,256,1024]{2,1,0:T(8,128)(2,1)} %bitcast.13), custom_call_target="tpu_custom_call" | custom-call | tf_op jit(solution)/shard_map/tail/pallas_call | solution.py:1203
  320.0 8.2 %finish.1 = (f32[8,1024]{1,0:T(8,128)}, f32[8,1024]{1,0:T(8,128)}, f32[1024,1024]{1,0:T(8,128)}, bf16[1024,1024]{1,0:T(8,128)(2,1)}, f32[128,3072]{1,0:T(8,128)}...) custom-call(bf16[32,512]{1,0:T(8,128)(2,1)} %get-tuple-element.73.refs_0_, ...), custom_call_target="tpu_custom_call" | custom-call | tf_op jit(solution)/shard_map/finish/pallas_call | solution.py:1268
Async XLA Ops:
  34.6 25.0 %collective-permute-start = (bf16[256,1024]{1,0:T(8,128)(2,1)}, bf16[256,1024]{1,0:T(8,128)(2,1)S(1)}, u32[]{:S(2)}, u32[]{:S(2)}) collective-permute-start(bf16[256,1024]{1,0:T(8,128)(2,1)} %get-tuple-element.53), channel_id=1, source_target_pairs={{0,8},{8,0},{16,24},{24,16},{1,9},{9,1},{17,25},{25,17},{2,10},{10... | collective-permute-start | bytes 1572872 | tf_op jit(solution)/shard_map/ppermute | solution.py:1283
  36.1 23.5 %collective-permute-start.1 = (bf16[256,1024]{1,0:T(8,128)(2,1)}, bf16[256,1024]{1,0:T(8,128)(2,1)}, u32[]{:S(2)}, u32[]{:S(2)}) collective-permute-start(bf16[256,1024]{1,0:T(8,128)(2,1)} %get-tuple-element.54), channel_id=1, source_target_pairs={{0,16},{8,24},{16,0},{24,8},{1,17},{9,25},{17,1},{25,9},{2,18},{10... | collective-permute-start | bytes 1572872 | tf_op jit(solution)/shard_map/ppermute | solution.py:1283
  37.6 22.0 %collective-permute-start.2 = (bf16[256,1024]{1,0:T(8,128)(2,1)}, bf16[256,1024]{1,0:T(8,128)(2,1)}, u32[]{:S(2)}, u32[]{:S(2)}) collective-permute-start(bf16[256,1024]{1,0:T(8,128)(2,1)} %get-tuple-element.55), channel_id=1, source_target_pairs={{0,24},{8,16},{16,8},{24,0},{1,25},{9,17},{17,9},{25,1},{2,26},{10... | collective-permute-start | bytes 1572872 | tf_op jit(solution)/shard_map/ppermute | solution.py:1283
  59.6 0.8 copy-start
